TPU v7x, 256 devices: a whole 4x4x8 slice. The times are simulated.
256 devices in a mesh: grp: 8 (over y, core), tp: 16 (over z, x_hi), sec: 2 (over x_lo).
Axes of the slice: x: 4 (x_hi: 2, x_lo: 2; x = x_hi * 2 + x_lo), y: 4, z: 8, core: 2. Of those that a mesh axis runs over, the one named last changes fastest.
Arguments:
- layer_in: bfloat16 [2, 512, 4, 8192], P('sec', 'grp', None, 'tp'), may hold values from -6 to 6
- q_weight: bfloat16 [2, 8192, 8192], P('sec', 'grp', 'tp'), may hold values from -0.0625 to 0.0625
- kv_weight: bfloat16 [2, 8192, 2048], P('sec', 'grp', 'tp'), may hold values from -0.0625 to 0.0625
- o_weight: bfloat16 [2, 8192, 8192], P('sec', 'tp', 'grp'), may hold values from -0.5 to 0.5
- kv_cache: bfloat16 [2, 512, 4096, 256], P('sec', 'grp', 'tp'), may hold values from -600 to 600
- cache_lengths: int32 [512], P('grp'), may hold values from 1 to 512, as said below
- value_head: float32 [8192], P('tp'), may hold values from -0.0625 to 0.0625
Outputs:
- hidden_out: bfloat16 [2, 512, 4, 8192], P('sec', 'grp', None, 'tp')
- token_gap: float32 [512, 4], P('grp', 'sec')
Inputs may be any that keep to these rules, and one draw needn't show every extreme that they name: `cache_lengths`: every rollout has at least one cached position; some rollout fills the whole cache and some holds a single position. Positions at or after a rollout's length hold arbitrary values.
All inputs are finite; a program needn't handle non-finite values.
Results may differ from a plain program's by a relative error of at most 0.018.
Values may be sent and summed in bfloat16 or wider, within the bound.
A program may use at most 128 MiB of HBM per device.

v0:
```python
import jax
import jax.numpy as jnp
from jax import lax
from jax.sharding import PartitionSpec as P

KVH = 8
HD = 128
CACHE = 512


def from_partner(value, axis, bit):
    mask = 2**bit
    pairs = [(source, source ^ mask) for source in range(lax.axis_size(axis))]
    return lax.ppermute(value, axis, pairs)


def local(layer_in, q_weight, kv_weight, o_weight, kv_cache, cache_lengths, value_head):
    tp_count = lax.axis_size("tp")
    tp_place = lax.axis_index("tp")
    sec_count = lax.axis_size("sec")
    sec_place = lax.axis_index("sec")
    rollouts = layer_in.shape[1]
    new_steps = layer_in.shape[2]
    tokens = rollouts * new_steps
    local_in = layer_in[0].reshape(tokens, layer_in.shape[3])
    full_in = lax.all_gather(local_in, "tp", axis=1, tiled=True)
    query_local = q_weight[0]
    pair_local = kv_weight[0]

    def add_rows(piece):
        return jnp.dot(full_in, piece, preferred_element_type=jnp.float32)

    query_sum = add_rows(lax.all_gather(query_local, "grp", axis=0, tiled=True))
    pair_sum = add_rows(lax.all_gather(pair_local, "grp", axis=0, tiled=True))
    query_vals = query_sum.astype(jnp.bfloat16)
    pair_vals = pair_sum.astype(jnp.bfloat16)
    pair_size = max(tp_count // KVH, 1)
    is_even = tp_place % 2 == 0
    query_other, pair_other = from_partner((query_vals, pair_vals), "tp", 0)
    query_low = jnp.where(is_even, query_vals, query_other)
    query_high = jnp.where(is_even, query_other, query_vals)
    query_all = jnp.concatenate([query_low, query_high], axis=1)
    local_heads = 1
    new_key = jnp.where(is_even, pair_vals, pair_other).reshape(rollouts, new_steps, 1, HD)
    new_value = jnp.where(is_even, pair_other, pair_vals).reshape(rollouts, new_steps, 1, HD)
    groups = query_all.shape[1] // (local_heads * HD)
    query_five = query_all.reshape(rollouts, new_steps, local_heads, groups, HD)
    rows_dev = kv_cache.shape[2]
    span = rows_dev // local_heads
    start_pos = tp_place * rows_dev % CACHE
    cache_five = kv_cache[0].reshape(rollouts, local_heads, span, 2, HD)
    cache_keys = cache_five[:, :, :, 0, :]
    cache_vals = cache_five[:, :, :, 1, :]
    leader = tp_place % pair_size == 0
    visible = ((start_pos + jnp.arange(span))[None, :] < cache_lengths[:, None])[
        :, None, None, None, :
    ]
    causal = (jnp.arange(new_steps)[None, :] <= jnp.arange(new_steps)[:, None]) & leader
    causal = causal[None, :, None, None, :]
    score_scale = HD ** (-0.5)
    cache_scores = (
        jnp.einsum("rskgd,rkpd->rskgp", query_five, cache_keys, preferred_element_type=jnp.float32)
        * score_scale
    )
    new_scores = (
        jnp.einsum("rskgd,rtkd->rskgt", query_five, new_key, preferred_element_type=jnp.float32)
        * score_scale
    )
    row_peak = jnp.maximum(
        jnp.max(jnp.where(visible, cache_scores, -1e30), axis=-1),
        jnp.max(jnp.where(causal, new_scores, -1e30), axis=-1),
    )
    cache_w = jnp.where(visible, jnp.exp(cache_scores - row_peak[..., None]), 0.0)
    new_w = jnp.where(causal, jnp.exp(new_scores - row_peak[..., None]), 0.0)
    row_total = jnp.sum(cache_w, axis=-1) + jnp.sum(new_w, axis=-1)
    weighted = jnp.einsum(
        "rskgp,rkpd->rskgd",
        cache_w.astype(jnp.bfloat16),
        cache_vals,
        preferred_element_type=jnp.float32,
    )
    weighted = weighted + jnp.einsum(
        "rskgt,rtkd->rskgd",
        new_w.astype(jnp.bfloat16),
        new_value,
        preferred_element_type=jnp.float32,
    )
    own_heads = groups // 2
    low_part = (
        row_peak[:, :, :, :own_heads],
        row_total[:, :, :, :own_heads],
        weighted[:, :, :, :own_heads],
    )
    high_part = (
        row_peak[:, :, :, own_heads:],
        row_total[:, :, :, own_heads:],
        weighted[:, :, :, own_heads:],
    )
    send_part = tuple(
        (jnp.where(is_even, high_one, low_one) for low_one, high_one in zip(low_part, high_part))
    )
    keep_part = tuple(
        (jnp.where(is_even, low_one, high_one) for low_one, high_one in zip(low_part, high_part))
    )
    got_part = (
        from_partner(send_part[0].astype(jnp.bfloat16), "tp", 0).astype(jnp.float32),
        from_partner(send_part[1].astype(jnp.bfloat16), "tp", 0).astype(jnp.float32),
        from_partner(send_part[2].astype(jnp.bfloat16), "tp", 0).astype(jnp.float32),
    )
    merged_peak = jnp.maximum(keep_part[0], got_part[0])
    own_factor = jnp.exp(keep_part[0] - merged_peak)
    far_factor = jnp.exp(got_part[0] - merged_peak)
    row_total = keep_part[1] * own_factor + got_part[1] * far_factor
    weighted = keep_part[2] * own_factor[..., None] + got_part[2] * far_factor[..., None]
    context = (weighted / row_total[..., None]).astype(jnp.bfloat16).reshape(tokens, -1)
    head_terms = jnp.dot(
        context,
        lax.all_gather(o_weight[0], "grp", axis=1, tiled=True),
        preferred_element_type=jnp.float32,
    )
    result = lax.psum_scatter(
        head_terms.astype(jnp.bfloat16), "tp", scatter_dimension=1, tiled=True
    )
    other_result = from_partner(result, "sec", 0)
    policy_part = jnp.where(sec_place == 0, result, other_result).astype(jnp.float32)
    refer_part = jnp.where(sec_place == 0, other_result, result).astype(jnp.float32)
    local_gap = jnp.sum((policy_part - refer_part) * value_head, axis=1)
    token_gap = lax.psum(local_gap, "tp")
    hidden_out = result.reshape(1, rollouts, new_steps, result.shape[1])
    gap_grid = token_gap.reshape(rollouts, new_steps)
    step_share = new_steps // sec_count
    own_gap = lax.dynamic_slice_in_dim(gap_grid, sec_place * step_share, step_share, 1)
    return (hidden_out, own_gap)


def solution(mesh):
    placed = (
        P("sec", "grp", None, "tp"),
        P("sec", "grp", "tp"),
        P("sec", "grp", "tp"),
        P("sec", "tp", "grp"),
        P("sec", "grp", "tp", None),
        P("grp"),
        P("tp"),
    )
    return jax.shard_map(
        local,
        mesh=mesh,
        in_specs=placed,
        out_specs=(P("sec", "grp", None, "tp"), P("grp", "sec")),
        check_vma=False,
    )
```

profile of v0, /device:TPU:8, one launch (start us, length us, event | category | flops | bytes accessed | tf_op | source)
XLA Modules:
  0.0 563.6 jit_solution(2793352173244113551)
XLA Ops:
  7.2 0.0 all-gather.12.cloned.1.call-start
  7.2 0.7 all-gather.12.cloned.1.call-update
  7.9 0.0 all-gather.8.cloned.1.call-start
  7.9 1.7 reshape_squeeze.6
  9.7 0.0 all-gather.8.cloned.1.call-update
  9.7 0.0 all-gather.10.cloned.1.call-start
  9.7 0.7 all-gather.10.cloned.1.call-update
  10.4 0.0 all-gather.14.cloned.1.call-start
  10.5 0.5 all-gather.14.cloned.1.call-update
  11.0 0.0 reduce-scatter.2.cloned.1.call-start
  11.1 0.7 broadcast_compare_fusion
  11.8 27.7 %all-gather.12.cloned.1.call-done = bf16[1,8192,128]{2,1,0:T(8,128)(2,1)} async-done(((bf16[1,1024,128]{2,1,0:T(8,128)(2,1)}), bf16[1,8192,128]{2,1,0:T(8,128)(2,1)}) %all-gather.12.cloned.1.call-update) | async-done | bytes 2097168 | tf_op jit(solution)/shard_map/all_gather | solution.py:34
  39.6 109.6 %all-gather.8.cloned.1.call-done = bf16[256,8192]{1,0:T(8,128)(2,1)} async-done(((bf16[256,512]{1,0:T(8,128)(2,1)}), bf16[256,8192]{1,0:T(8,128)(2,1)}) %all-gather.8.cloned.1.call-update) | async-done | bytes 4194320 | tf_op jit(solution)/shard_map/all_gather | solution.py:26
  149.2 4.1 fusion.16
  153.3 0.6 collective-permute-start.1
  154.0 45.2 %all-gather.10.cloned.1.call-done = bf16[1,8192,512]{2,1,0:T(8,128)(2,1)} async-done(((bf16[1,1024,512]{2,1,0:T(8,128)(2,1)}), bf16[1,8192,512]{2,1,0:T(8,128)(2,1)}) %all-gather.10.cloned.1.call-update) | async-done | bytes 8388624 | tf_op jit(solution)/shard_map/all_gather | solution.py:33
  199.1 7.0 %fusion.13 = bf16[256,512]{1,0:T(8,128)(2,1)S(1)} fusion(bf16[256,8192]{1,0:T(8,128)(2,1)} %all-gather.8.cloned.1.call-done, bf16[1,8192,512]{2,1,0:T(8,128)(2,1)} %all-gather.10.cloned.1.call-done), kind=kOutput, calls=%fused_computation.22 | convolution fusion | flops 2147614720 | bytes 12845056 | tf_op jit(solution)/shard_map/dot_general | solution.py:31
  206.1 3.1 collective-permute-start
  209.2 11.7 %copy.9 = bf16[1,64,256,256]{2,3,1,0:T(8,128)(2,1)} copy(bf16[1,64,256,256]{3,2,1,0:T(8,128)(2,1)} %param.11) | data formatting | bytes 16777216 | tf_op args[4]
  220.9 0.0 collective-permute-done.1
  220.9 0.0 collective-permute-done
  220.9 0.0 slice-start
  221.0 0.1 maximum_bitcast_fusion
  221.0 0.1 copy.19
  221.1 2.4 select_reduce_fusion
  223.6 0.0 slice-start.1
  223.6 3.3 fusion.7
  227.0 0.5 fusion.26
  227.5 0.9 bitcast_reduce_fusion
  228.4 0.1 select_convert_fusion.1
  228.5 0.9 collective-permute-start.4
  229.5 0.1 select_convert_fusion.2
  229.6 2.8 collective-permute-start.2
  232.4 0.0 slice-done
  232.4 0.0 slice-done.1
  232.4 1.6 fusion.10
  234.0 0.5 fusion.11
  234.5 0.2 select_convert_fusion
  234.7 1.1 collective-permute-start.3
  235.8 0.1 collective-permute-done.2
  235.9 0.1 fusion.38
  236.0 0.0 collective-permute-done.4
  236.0 0.2 fusion.37
  236.2 8.3 %collective-permute-done.3 = bf16[64,4,1,4,128]{4,3,1,0,2:T(4,128)(2,1)S(1)} collective-permute-done((bf16[64,4,1,4,128]{4,3,1,0,2:T(4,128)(2,1)S(1)}, bf16[64,4,1,4,128]{4,3,1,0,2:T(4,128)(2,1)S(1)}, u32[]{:S(2)}, u32[]{:S(2)}) %collective-permute-start.3) | collective-permute-done | bytes 262176 | tf_op jit(solution)/shard_map/ppermute | solution.py:14
  244.5 1.0 fusion.25
  245.4 7.9 %all-gather.14.cloned.1.call-done = bf16[1,512,8192]{2,1,0:T(8,128)(2,1)} async-done(((bf16[1,512,1024]{2,1,0:T(8,128)(2,1)}), bf16[1,512,8192]{2,1,0:T(8,128)(2,1)}) %all-gather.14.cloned.1.call-update) | async-done | bytes 8388624 | tf_op jit(solution)/shard_map/all_gather | solution.py:118
  253.3 7.7 %convolution_convert_fusion = bf16[256,8192]{1,0:T(8,128)(2,1)} fusion(bf16[1,512,8192]{2,1,0:T(8,128)(2,1)} %all-gather.14.cloned.1.call-done, bf16[32,8,4,128]{3,2,1,0:T(4,128)(2,1)S(1)} %bitcast.117), kind=kOutput, calls=%fused_computation | convolution fusion | flops 2149580800 | bytes 12845056 | tf_op jit(solution)/shard_map/dot_general | solution.py:116
  261.0 0.0 copy-start
  261.0 0.0 reduce-scatter.2.cloned.1.call-update
  261.1 213.8 %reduce-scatter.2.cloned.1.call-done = bf16[256,512]{1,0:T(8,128)(2,1)} async-done(((bf16[256,8192]{1,0:T(8,128)(2,1)}), bf16[256,512]{1,0:T(8,128)(2,1)}) %reduce-scatter.2.cloned.1.call-update) | async-done | bytes 262160 | tf_op jit(solution)/shard_map/reduce_scatter | solution.py:121
  474.9 0.5 collective-permute-start.5
  475.4 1.8 reshape.158
  477.2 4.3 collective-permute-done.5
  481.5 0.0 copy-done
  481.5 1.1 multiply_reduce_fusion
  482.6 0.1 reshape.159
  482.7 73.6 %psum.7 = f32[64,4]{1,0:T(8,128)S(1)} all-reduce(f32[64,4]{1,0:T(8,128)S(1)} %reshape.159), channel_id=1, replica_groups=mesh['grp'=8,'tp'=16,'sec'=2] {'tp'}, use_global_device_ids=true, to_apply=%region_6.7 | all-reduce | flops 256 | bytes 2048 | tf_op jit(solution)/shard_map/psum | solution.py:128
  556.3 0.1 constant_dynamic-slice_fusion
  556.4 0.6 copy.12
  (7 shorter events, 0.1 us)
Async XLA Ops:
  7.2 32.4 %all-gather.12.cloned.1.call-start = ((), (), s32[]{:S(2)}) async-start(), calls=%async_computation.4 | async-start | bytes 2359296 | tf_op jit(solution)/shard_map/all_gather | solution.py:34
  7.9 141.3 %all-gather.8.cloned.1.call-start = ((), (), s32[]{:S(2)}) async-start(), calls=%async_computation.1 | async-start | bytes 4456448 | tf_op jit(solution)/shard_map/all_gather | solution.py:26
  9.7 189.4 %all-gather.10.cloned.1.call-start = ((), (), s32[]{:S(2)}) async-start(), calls=%async_computation.3 | async-start | bytes 9437184 | tf_op jit(solution)/shard_map/all_gather | solution.py:33
  10.4 242.9 %all-gather.14.cloned.1.call-start = ((), (), s32[]{:S(2)}) async-start(), calls=%async_computation.5 | async-start | bytes 9437184 | tf_op jit(solution)/shard_map/all_gather | solution.py:118
  11.0 463.9 %reduce-scatter.2.cloned.1.call-start = ((), (), s32[]{:S(2)}) async-start(), calls=%async_computation.2 | async-start | bytes 4456448 | tf_op jit(solution)/shard_map/reduce_scatter | solution.py:121
  153.3 67.6 %collective-permute-start.1 = (bf16[256,128]{1,0:T(8,128)(2,1)S(1)}, bf16[256,128]{1,0:T(8,128)(2,1)S(1)}, u32[]{:S(2)}, u32[]{:S(2)}) collective-permute-start(bf16[256,128]{1,0:T(8,128)(2,1)S(1)} %fusion.16), channel_id=1, source_target_pairs={{0,2},{2,0},{4,6},{6,4},{8,10},{10,8},{12,14},{14,12},{16,18},{18,... | collective-permute-start | bytes 196616 | tf_op jit(solution)/shard_map/ppermute | solution.py:14
  206.1 14.8 %collective-permute-start = (bf16[256,512]{1,0:T(8,128)(2,1)S(1)}, bf16[256,512]{1,0:T(8,128)(2,1)S(1)}, u32[]{:S(2)}, u32[]{:S(2)}) collective-permute-start(bf16[256,512]{1,0:T(8,128)(2,1)S(1)} %fusion.13), channel_id=1, source_target_pairs={{0,2},{2,0},{4,6},{6,4},{8,10},{10,8},{12,14},{14,12},{16,18},{18,... | collective-permute-start | bytes 786440 | tf_op jit(solution)/shard_map/ppermute | solution.py:14
  220.9 11.5 %slice-start = ((s8[8388608]{0:T(1024)(128)(4,1)}), s8[4194304]{0:T(1024)(128)(4,1)S(1)}, s32[]{:S(2)}) async-start(s8[8388608]{0:T(1024)(128)(4,1)} %bitcast.110), calls=%async_computation.6 | async-start | bytes 8388608
  223.6 8.8 %slice-start.1 = ((s8[8388608]{0:T(1024)(128)(4,1)}), s8[4194304]{0:T(1024)(128)(4,1)S(1)}, s32[]{:S(2)}) async-start(s8[8388608]{0:T(1024)(128)(4,1)} %bitcast.110), calls=%async_computation.7 | async-start | bytes 8388608
  228.5 7.5 %collective-permute-start.4 = (bf16[64,4,1,4]{3,1,0,2:T(4,128)(2,1)S(1)}, bf16[64,4,1,4]{3,1,0,2:T(4,128)(2,1)S(1)}, u32[]{:S(2)}, u32[]{:S(2)}) collective-permute-start(bf16[64,4,1,4]{3,1,0,2:T(4,128)(2,1)S(1)} %select_convert_fusion.1), channel_id=1, source_target_pairs={{0,2},{2,0},{4,6},{6,4},{8,10},{10,8},{12,14},{14,12},{16,18},{18,... | collective-permute-start | bytes 6152 | tf_op jit(solution)/shard_map/ppermute | solution.py:14
  229.6 6.3 %collective-permute-start.2 = (bf16[64,4,1,4]{3,1,0,2:T(4,128)(2,1)S(1)}, bf16[64,4,1,4]{3,1,0,2:T(4,128)(2,1)S(1)}, u32[]{:S(2)}, u32[]{:S(2)}) collective-permute-start(bf16[64,4,1,4]{3,1,0,2:T(4,128)(2,1)S(1)} %select_convert_fusion.2), channel_id=1, source_target_pairs={{0,2},{2,0},{4,6},{6,4},{8,10},{10,8},{12,14},{14,12},{16,18},{18,... | collective-permute-start | bytes 6152 | tf_op jit(solution)/shard_map/ppermute | solution.py:14
  234.7 9.8 %collective-permute-start.3 = (bf16[64,4,1,4,128]{4,3,1,0,2:T(4,128)(2,1)S(1)}, bf16[64,4,1,4,128]{4,3,1,0,2:T(4,128)(2,1)S(1)}, u32[]{:S(2)}, u32[]{:S(2)}) collective-permute-start(bf16[64,4,1,4,128]{4,3,1,0,2:T(4,128)(2,1)S(1)} %select_convert_fusion), channel_id=1, source_target_pairs={{0,2},{2,0},{4,6},{6,4},{8,10},{10,8},{12,14},{14,12},{16,18},{18,... | collective-permute-start | bytes 786440 | tf_op jit(solution)/shard_map/ppermute | solution.py:14
  261.0 220.4 %copy-start = (f32[512]{0:T(512)S(1)}, f32[512]{0:T(512)}, u32[]{:S(2)}) copy-start(f32[512]{0:T(512)} %param.13) | copy-start | bytes 6148
  474.9 6.6 %collective-permute-start.5 = (bf16[256,512]{1,0:T(8,128)(2,1)}, bf16[256,512]{1,0:T(8,128)(2,1)S(1)}, u32[]{:S(2)}, u32[]{:S(2)}) collective-permute-start(bf16[256,512]{1,0:T(8,128)(2,1)} %reduce-scatter.2.cloned.1.call-done), channel_id=1, source_target_pairs={{0,1},{1,0},{2,3},{3,2},{4,5},{5,4},{6,7},{7,6},{8,9},{9,8},{10,11... | collective-permute-start | bytes 786440 | tf_op jit(solution)/shard_map/ppermute | solution.py:14
Sparse Core Ops, SparseCore 0:
  9.9 29.6 all-gather.11
  42.6 106.5 all-gather.7
  151.1 48.0 all-gather.9
  200.8 52.4 all-gather.13
  261.2 213.6 reduce-scatter.1
where the time goes:
time: 564 us
  waiting for transfers between devices  419 us (74%)
  blocking collectives  73.6 us (13%)
  matrix products  26.7 us (5%)
  local copies, waits for them, and re-layouts  16.1 us (3%)
  between operations  14 us (2%)
  starting transfers between devices  9.26 us (2%)
    reduce_scatter x1, waiting for transfers between devices, local(): lax.psum_scatter(head_terms.astype(jnp.bfloat16), 'tp', scatter_dimension...  214 us
    all_gather x1, waiting for transfers between devices, local(): full_in = lax.all_gather(local_in, 'tp', axis=1, tiled=True)  110 us
    psum x1, blocking collectives, local(): token_gap = lax.psum(local_gap, 'tp')  73.6 us
    all_gather x1, waiting for transfers between devices, local(): query_sum = add_rows(lax.all_gather(query_local, 'grp', axis=0, tiled=True))  45.2 us
    all_gather x1, waiting for transfers between devices, local(): pair_sum = add_rows(lax.all_gather(pair_local, 'grp', axis=0, tiled=True))  27.7 us
    ppermute x6, waiting for transfers between devices, from_partner(): return lax.ppermute(value, axis, pairs)  12.6 us
    unnamed x9, local copies, waits for them, and re-layouts  12.4 us
  transfers between devices with their start and end apart: 11, of which 8 were waited for; matrix products, arithmetic and copies ran while one was open for 7% of the time, Pallas kernels for 0%

commit v1 on v0

v1 whole, which is shorter than its diff:
```python
import functools

import jax
import jax.numpy as jnp
from jax import lax
from jax.experimental import pallas as pl
from jax.experimental.pallas import tpu as pltpu
from jax.sharding import PartitionSpec as P

HD = 128
CACHE = 512
MESH = pl.DeviceIdType.MESH
BF = jnp.bfloat16
F32 = jnp.float32
MIB = 1024 * 1024


def dot(a, b):
    return jnp.dot(a, b, preferred_element_type=F32)


def dot_nt(a, b):
    return lax.dot_general(a, b, (((1,), (1,)), ((), ())), preferred_element_type=F32)


def remote(src, dst, send, recv, **where):
    return pltpu.make_async_remote_copy(
        src_ref=src, dst_ref=dst, send_sem=send, recv_sem=recv, device_id=where, device_id_type=MESH
    )


def places():
    grp, tp = lax.axis_index("grp"), lax.axis_index("tp")
    return grp, tp, grp // 2, grp % 2, tp // 2, tp % 2


class OutputWeights:
    def __init__(self, src, full, y_send, y_recv, c_send, c_recv, own_sem):
        grp, tp, y, c, z, xh = places()
        self.grp, self.c, self.y = grp, c, y
        self.right, self.left = 2 * ((y + 1) % 4) + c, 2 * ((y + 3) % 4) + c
        self.src, self.full = src, full
        self.y_send, self.y_recv, self.c_send, self.c_recv, self.own_sem = y_send, y_recv, c_send, c_recv, own_sem

    def to_core(self, slot, src, place):
        return remote(src, self.full.at[place], self.c_send.at[slot], self.c_recv.at[slot], grp=self.grp ^ 1)

    def from_core(self, slot, place):
        return remote(
            self.full.at[place], self.full.at[place ^ 1], self.c_send.at[slot], self.c_recv.at[slot], grp=self.grp ^ 1
        )

    def one(self, which, place, src=None):
        to = self.right if which == 0 else self.left
        return remote(
            self.full.at[place] if src is None else src, self.full.at[place],
            self.y_send.at[which], self.y_recv.at[which], grp=to,
        )

    def half(self, which, place):
        to = self.right if which == 0 else self.left
        rows = pl.ds(256 * which, 256)
        return remote(
            self.full.at[place, rows], self.full.at[place, rows],
            self.y_send.at[2 + which], self.y_recv.at[2 + which], grp=to,
        )

    def start(self):
        self.own = pltpu.make_async_copy(self.src, self.full.at[self.grp], self.own_sem)
        self.own.start()
        self.sent = [self.one(0, self.grp, self.src), self.one(1, self.grp, self.src), self.to_core(0, self.src, self.grp)]
        for copy in self.sent:
            copy.start()

    def middle(self):
        for which, place in ((0, self.left), (1, self.right)):
            self.one(which, place).wait_recv()
            ahead = self.half(which, place)
            ahead.start()
            over = self.to_core(1 + which, self.full.at[place], place)
            over.start()
            self.sent += [ahead, over]

    def last(self):
        far = 2 * ((self.y + 2) % 4) + self.c
        for which in (0, 1):
            self.half(which, far).wait_recv()
        over = self.to_core(3, self.full.at[far], far)
        over.start()
        self.sent.append(over)

    def finish(self):
        self.own.wait()
        for copy in self.sent:
            copy.wait_send()
        for slot in range(4):
            self.from_core(slot, self.grp).wait_recv()


def project_kernel(
    x_hbm, wq_hbm, wkv_hbm, wo_hbm, qkv_out, wo_own, wo_far,
    xs, ws, mine, keep, to_core, from_core, to_y, from_y, final,
    perm_send, perm_recv, r_send, r_recv, l_send, l_recv, w_local, w_send, w_recv,
    c_send, c_recv, y_send, y_recv, a_send, a_recv, b_send, b_recv, own_sem,
    g_send, g_recv, h_send, h_recv, g_own, f_send, f_recv,
):
    grp, tp, y, c, z, xh = places()
    ring_r, ring_l = 2 * ((z + 1) % 8) + xh, 2 * ((z + 7) % 8) + xh
    dst_grp, dst_tp = z, 2 * (2 * y + xh) + c
    src_grp, src_tp = 2 * (z // 2) + xh, 2 * grp + z % 2
    stays = (dst_grp == grp) & (dst_tp == tp)
    moves = jnp.logical_not(stays)

    barrier = pltpu.get_barrier_semaphore()

    def greet(**where):
        pl.semaphore_signal(barrier, inc=1, device_id=where, device_id_type=MESH)

    @pl.when(moves)
    def _():
        greet(grp=dst_grp, tp=dst_tp)
        greet(grp=src_grp, tp=src_tp)

    greet(tp=ring_r)
    greet(tp=ring_l)
    greet(tp=tp ^ 1)
    greet(grp=grp ^ 1)
    greet(grp=grp ^ 1, tp=tp ^ 1)
    for d in (1, 2, 3):
        greet(grp=2 * ((y + d) % 4) + c)
    pl.semaphore_wait(barrier, jnp.where(moves, 10, 8))

    def rows(ch):
        return pl.ds(128 * ch, 128)

    def perm(ch):
        return remote(
            x_hbm.at[rows(ch)], xs.at[2 * y + xh, rows(ch)], perm_send.at[ch], perm_recv.at[ch], grp=dst_grp, tp=dst_tp
        )

    def perm_local(ch):
        return pltpu.make_async_copy(x_hbm.at[rows(ch)], xs.at[z, rows(ch)], perm_recv.at[ch])

    for ch in (0, 1):
        pl.when(moves)(lambda ch=ch: perm(ch).start())
        pl.when(stays)(lambda ch=ch: perm_local(ch).start())

    w_out = [
        remote(wq_hbm, ws.at[1, :, pl.ds(0, 512)], w_send.at[0], w_recv.at[0], tp=tp ^ 1),
        remote(wkv_hbm, ws.at[1, :, pl.ds(512, 128)], w_send.at[1], w_recv.at[1], tp=tp ^ 1),
    ]
    w_in = [
        pltpu.make_async_copy(wq_hbm, ws.at[0, :, pl.ds(0, 512)], w_local.at[0]),
        pltpu.make_async_copy(wkv_hbm, ws.at[0, :, pl.ds(512, 128)], w_local.at[1]),
    ]
    for copy in w_out + w_in:
        copy.start()
    wo = OutputWeights(
        wo_hbm.at[:, pl.ds(pl.multiple_of(512 * xh, 512), 512)], wo_own, g_send, g_recv, h_send, h_recv, g_own.at[0]
    )
    wo.start()

    def ring(right, k, ch, place):
        ss, rs, to = (r_send, r_recv, ring_r) if right else (l_send, l_recv, ring_l)
        block = xs.at[place, rows(ch)]
        return remote(block, block, ss.at[k - 1, ch], rs.at[k - 1, ch], tp=to)

    sent = []

    def send(copy):
        copy.start()
        sent.append(copy)

    def travels(right, k, ch):
        return k < 4 or (k == 4 and ch == (0 if right else 1))

    for ch in (0, 1):
        pl.when(moves)(lambda ch=ch: remote(
            x_hbm.at[rows(ch)], xs.at[z, rows(ch)], perm_send.at[ch], perm_recv.at[ch], grp=dst_grp, tp=dst_tp
        ).wait_recv())
        pl.when(stays)(lambda ch=ch: perm_local(ch).wait())
        for right in (True, False):
            send(ring(right, 1, ch, z))

    even = z % 2 == 0
    pair = z // 2
    order = [
        pair,
        jnp.where(even, pair + 3, pair + 1) % 4,
        jnp.where(even, pair + 1, pair + 3) % 4,
        (pair + 2) % 4,
    ]

    def product(j, yp, half):
        block = pl.ds(pl.multiple_of(128 * half, 128), 128)
        return dot(xs[2 * yp, block, :], ws[j, :512, :]) + dot(xs[2 * yp + 1, block, :], ws[j, 512:, :])

    def core_copy(j, i):
        return remote(to_core.at[j, i], from_core.at[j, i], c_send.at[j, i], c_recv.at[j, i], grp=grp ^ 1)

    def compute(j, i):
        to_core[j, i] = product(j, order[i], c ^ 1).astype(BF)
        send(core_copy(j, i))
        mine[j, i] = product(j, order[i], c)

    def y_copy(j, i, d):
        return remote(
            to_y.at[j, i], from_y.at[j, d - 1], y_send.at[j, i], y_recv.at[j, d - 1],
            grp=2 * ((y + d) % 4) + c,
        )

    def pass_on(j, i):
        core_copy(j, i).wait_recv()
        total = mine[j, i] + from_core[j, i].astype(F32)
        d = (order[i] - y + 4) % 4

        @pl.when(d == 0)
        def _():
            keep[j] = total

        @pl.when(d != 0)
        def _():
            to_y[j, i] = total.astype(BF)
            y_copy(j, i, d).start()

    for copy in w_in:
        copy.wait()
    for k in (1, 2, 3, 4):
        for ch in (0, 1):
            for right in (True, False):
                if not travels(right, k, ch):
                    continue
                place = (z + 8 - k) % 8 if right else (z + k) % 8
                ring(right, k, ch, place).wait_recv()
                if k < 4 and travels(right, k + 1, ch):
                    send(ring(right, k + 1, ch, place))
        compute(0, k - 1)
        if k > 1:
            pass_on(0, k - 2)
        if k == 2:
            wo.middle()
    pass_on(0, 3)
    for copy in w_out:
        copy.wait_recv()
    far_cols = pl.ds(pl.multiple_of(512 * (xh ^ 1), 512), 512)
    far = remote(wo_hbm.at[:, far_cols], wo_far, f_send.at[0], f_recv.at[0], tp=tp ^ 1)
    far.start()
    for i in range(4):
        compute(1, i)
        if i > 0:
            pass_on(1, i - 1)
    pass_on(1, 3)
    wo.last()

    near = c == xh

    def place_of(cols, half):
        return qkv_out.at[cols, pl.ds(pl.multiple_of(128 * half, 128), 128)]

    for j in (0, 1):
        total = keep[j]
        for d in (1, 2, 3):
            remote(to_y.at[j, 0], from_y.at[j, d - 1], y_send.at[j, 0], y_recv.at[j, d - 1], grp=grp).wait_recv()
            total = total + from_y[j, d - 1].astype(F32)
        final[j] = total.astype(BF)
        spot = place_of(xh ^ j, c)

        @pl.when(near)
        def _():
            pltpu.make_async_copy(final.at[j], spot, own_sem.at[j]).start()

        @pl.when(jnp.logical_not(near))
        def _():
            remote(final.at[j], spot, a_send.at[j], a_recv.at[j], grp=grp ^ 1).start()

        remote(final.at[j], spot, b_send.at[j], b_recv.at[j, c], grp=2 * y + xh, tp=tp ^ 1).start()

    for j in (0, 1):
        spot = place_of(xh ^ j, c)

        @pl.when(near)
        def _():
            pltpu.make_async_copy(final.at[j], spot, own_sem.at[j]).wait()
            remote(final.at[j], place_of(xh ^ j, c ^ 1), a_send.at[j], a_recv.at[j], grp=grp ^ 1).wait_recv()

        @pl.when(jnp.logical_not(near))
        def _():
            remote(final.at[j], spot, a_send.at[j], a_recv.at[j], grp=grp ^ 1).wait_send()
            for half in (0, 1):
                remote(
                    final.at[j], place_of(xh ^ 1 ^ j, half), b_send.at[j], b_recv.at[j, half],
                    grp=2 * y + xh, tp=tp ^ 1,
                ).wait_recv()

        remote(final.at[j], spot, b_send.at[j], b_recv.at[j, c], grp=2 * y + xh, tp=tp ^ 1).wait_send()

    for copy in sent:
        copy.wait_send()
    for copy in w_out:
        copy.wait_send()
    for ch in (0, 1):
        pl.when(moves)(lambda ch=ch: perm(ch).wait_send())
    for j in (0, 1):
        for i in range(4):
            d = (order[i] - y + 4) % 4
            pl.when(d != 0)(lambda j=j, i=i, d=d: y_copy(j, i, d).wait_send())
    wo.finish()
    far.wait()


def project(x, wq, wkv, wo):
    dma = pltpu.SemaphoreType.DMA
    anywhere = pl.BlockSpec(memory_space=pl.ANY)
    return pl.pallas_call(
        project_kernel,
        out_shape=(
            jax.ShapeDtypeStruct((2, 256, 640), BF),
            jax.ShapeDtypeStruct((8, 512, 512), BF),
            jax.ShapeDtypeStruct((512, 512), BF),
        ),
        in_specs=[anywhere] * 4,
        out_specs=(anywhere,) * 3,
        scratch_shapes=[
            pltpu.VMEM((8, 256, 512), BF),
            pltpu.VMEM((2, 1024, 640), BF),
            pltpu.VMEM((2, 4, 128, 640), F32),
            pltpu.VMEM((2, 128, 640), F32),
            pltpu.VMEM((2, 4, 128, 640), BF),
            pltpu.VMEM((2, 4, 128, 640), BF),
            pltpu.VMEM((2, 4, 128, 640), BF),
            pltpu.VMEM((2, 3, 128, 640), BF),
            pltpu.VMEM((2, 128, 640), BF),
            dma((2,)), dma((2,)), dma((4, 2)), dma((4, 2)), dma((4, 2)), dma((4, 2)), dma((2,)), dma((2,)), dma((2,)),
            dma((2, 4)), dma((2, 4)), dma((2, 4)), dma((2, 3)), dma((2,)), dma((2,)), dma((2,)), dma((2, 2)), dma((2,)),
            dma((4,)), dma((4,)), dma((4,)), dma((4,)), dma((1,)), dma((1,)), dma((1,)),
        ],
        compiler_params=pltpu.CompilerParams(
            collective_id=0, has_side_effects=True, vmem_limit_bytes=40 * MIB
        ),
        name="project",
    )(x, wq, wkv, wo)


def attend_kernel(q_ref, kv_ref, len_ref, out_ref, lse_ref, q_rows):
    step = pl.program_id(0)
    leader = lax.axis_index("tp") % 2 == 0
    scale = HD ** -0.5
    lane = lax.broadcasted_iota(jnp.int32, (1, 128), 1)
    pos = lax.broadcasted_iota(jnp.int32, (256, 128), 0)
    lane_roll, lane_step = lane // 32, lane % 32 // 8
    new_row = lax.broadcasted_iota(jnp.int32, (16, 128), 0)
    causal = (new_row // 4 == lane_roll) & (new_row % 4 <= lane_step) & leader
    for group in range(2):
        tokens = pl.ds(16 * group, 16)
        for part in (0, 1):
            vals = q_ref[part, tokens, :].astype(F32)
            for head in range(4):
                q_rows[pl.ds(4 * part + head, 16, stride=8), :] = vals[:, 128 * head:128 * head + 128]
        new_key = q_ref[0, tokens, 512:]
        new_val = q_ref[1, tokens, 512:]
        q_t = q_rows[...].T.astype(BF)
        cached = None
        for i in range(4):
            one = dot(kv_ref[4 * group + i, :, :128], q_t)
            cached = one if cached is None else jnp.where(lane_roll == i, one, cached)
        visible = pos < len_ref[0, group:group + 1, :]
        cached = jnp.where(visible, cached * scale, -1e30)
        fresh = jnp.where(causal, dot(new_key, q_t) * scale, -1e30)
        peak = jnp.maximum(jnp.max(cached, axis=0, keepdims=True), jnp.max(fresh, axis=0, keepdims=True))
        cached = jnp.where(visible, jnp.exp(cached - peak), 0.0)
        fresh = jnp.where(causal, jnp.exp(fresh - peak), 0.0)
        total = jnp.sum(cached, axis=0, keepdims=True) + jnp.sum(fresh, axis=0, keepdims=True)
        lse_ref[0, group:group + 1, :] = jnp.where(total > 0.0, peak + jnp.log(jnp.maximum(total, 1e-30)), -1e30)
        inverse = jnp.where(total > 0.0, 1.0 / jnp.maximum(total, 1e-30), 0.0)
        weights = (cached * inverse).T.astype(BF)
        fresh_w = jnp.concatenate([fresh * inverse, jnp.zeros((112, 128), F32)], axis=0).T.astype(BF)
        new_pad = jnp.concatenate([new_val, jnp.zeros((112, 128), BF)], axis=0)
        added = dot(fresh_w, new_pad)
        for i in range(4):
            block = slice(32 * i, 32 * i + 32)
            got = dot(weights[block], kv_ref[4 * group + i, :, 128:]) + added[block]
            out_ref[pl.ds(128 * group + 32 * i, 32), :] = got.astype(BF)


def attend(qkv, cache, spans):
    return pl.pallas_call(
        attend_kernel,
        grid=(8,),
        out_shape=(jax.ShapeDtypeStruct((2048, 128), BF), jax.ShapeDtypeStruct((8, 2, 128), F32)),
        in_specs=[
            pl.BlockSpec((2, 32, 640), lambda i: (0, i, 0)),
            pl.BlockSpec((8, 256, 256), lambda i: (i, 0, 0)),
            pl.BlockSpec((1, 2, 128), lambda i: (i, 0, 0)),
        ],
        out_specs=(
            pl.BlockSpec((256, 128), lambda i: (i, 0)),
            pl.BlockSpec((1, 2, 128), lambda i: (i, 0, 0)),
        ),
        scratch_shapes=[pltpu.VMEM((128, 128), F32)],
        compiler_params=pltpu.CompilerParams(vmem_limit_bytes=16 * MIB),
        name="attend",
    )(qkv, cache, spans)


def finish_kernel(
    o_ref, lse_ref, wo_own_hbm, wo_far_hbm, head_ref, hidden_out, gap_out,
    o_got, lse_got, near_w, far_w, merged, ctx, outgo, income, gap_own, gap_x, gap_z,
    o_send, o_recv, s_send, s_recv, near_sem,
    g_send, g_recv, h_send, h_recv, g_own,
    ring_send, ring_recv, gx_send, gx_recv, gz_send, gz_recv,
):
    grp, tp, y, c, z, xh = places()
    sec = lax.axis_index("sec")
    barrier = pltpu.get_barrier_semaphore()

    def greet(**where):
        pl.semaphore_signal(barrier, inc=1, device_id=where, device_id_type=MESH)

    greet(tp=tp ^ 1)
    greet(sec=sec ^ 1)
    greet(tp=tp ^ 1, sec=sec ^ 1)
    greet(grp=grp ^ 1)
    for d in (1, 2, 3):
        greet(grp=2 * ((y + d) % 4) + c)
    for d in range(1, 8):
        greet(tp=2 * ((z + d) % 8) + xh)
    pl.semaphore_wait(barrier, 14)

    stats = remote(lse_ref, lse_got, s_send.at[0], s_recv.at[0], tp=tp ^ 1)
    stats.start()
    parts = []
    for n in range(4):
        block = pl.ds(512 * n, 512)
        parts.append(remote(o_ref.at[block], o_got.at[block], o_send.at[n], o_recv.at[n], tp=tp ^ 1))
        parts[-1].start()
    near = pltpu.make_async_copy(wo_own_hbm, near_w, near_sem.at[0])
    near.start()
    wo = OutputWeights(wo_far_hbm, far_w, g_send, g_recv, h_send, h_recv, g_own.at[0])
    wo.start()

    stats.wait_recv()
    for n in range(4):
        parts[n].wait_recv()
        for m in range(4 * n, 4 * n + 4):
            factor = 1.0 / (1.0 + jnp.exp(lse_got[m // 2, m % 2:m % 2 + 1, :] - lse_ref[m // 2, m % 2:m % 2 + 1, :]))
            factor = jnp.broadcast_to(factor, (128, 128)).T
            block = slice(128 * m, 128 * m + 128)
            own = o_ref[block, :].astype(F32)
            got = o_got[block, :].astype(F32)
            merged[block, :] = own * factor + got * (1.0 - factor)
        if n == 1:
            wo.middle()
    for part in (0, 1):
        for head in range(4):
            ctx[part, :, pl.ds(128 * head, 128)] = merged[pl.ds(4 * part + head, 256, stride=8), :].astype(BF)
    near.wait()
    wo.last()
    wo.finish()

    def block(place, ch):
        return dot(ctx[xh, 128 * ch:128 * ch + 128, :], near_w[place]) + dot(
            ctx[xh ^ 1, 128 * ch:128 * ch + 128, :], far_w[place]
        )

    def slot(right, ch):
        return 2 * ch + (0 if right else 1)

    def ring(right, ch, k):
        s = slot(right, ch)
        to = 2 * ((z + (1 if right else 7)) % 8) + xh
        return remote(outgo.at[s, k - 1], income.at[s, k - 1], ring_send.at[s, k - 1], ring_recv.at[s, k - 1], tp=to)

    sent = []

    def longest(right, ch):
        return 4 if ch == (0 if right else 1) else 3

    for turn in range(4):
        for right, ch in ((True, 0), (False, 1), (True, 1), (False, 0)):
            k = longest(right, ch) - turn
            if k < 1:
                continue
            place = (z + k) % 8 if right else (z + 8 - k) % 8
            total = block(place, ch)
            if turn > 0:
                ring(right, ch, k + 1).wait_recv()
                total = total + income[slot(right, ch), k].astype(F32)
            outgo[slot(right, ch), k - 1] = total.astype(BF)
            copy = ring(right, ch, k)
            copy.start()
            sent.append(copy)

    value = head_ref[...]
    first = value.astype(BF)
    rest = value - first.astype(F32)
    second = rest.astype(BF)
    third = (rest - second.astype(F32)).astype(BF)
    which = lax.broadcasted_iota(jnp.int32, (16, 512), 0)
    triple = jnp.where(
        which == 0, first.astype(F32),
        jnp.where(which == 1, second.astype(F32), jnp.where(which == 2, third.astype(F32), 0.0)),
    ).astype(BF)
    gaps = []
    for ch in (0, 1):
        total = block(z, ch)
        for right in (True, False):
            ring(right, ch, 1).wait_recv()
            total = total + income[slot(right, ch), 0].astype(F32)
        result = total.astype(BF)
        hidden_out[128 * ch:128 * ch + 128, :] = result
        gaps.append(jnp.sum(dot_nt(triple, result), axis=0, keepdims=True))
    gap = jnp.concatenate(gaps, axis=1)
    gap = jnp.where(sec == 0, gap, -gap)
    own_x = 2 * xh + sec
    gap_own[...] = jnp.broadcast_to(gap, (8, 256))

    def gap_far(d):
        return remote(
            gap_own, gap_x.at[own_x], gx_send.at[d - 1], gx_recv.at[d - 1], tp=tp ^ (d // 2), sec=sec ^ (d % 2)
        )

    for d in (1, 2, 3):
        gap_far(d).start()
    gap_x[own_x] = gap_own[...]
    for d in (1, 2, 3):
        gap_far(d).wait_recv()
    gap_z[z] = gap_x[0] + gap_x[1] + gap_x[2] + gap_x[3]

    def gap_ring(d):
        return remote(
            gap_z.at[z], gap_z.at[z], gz_send.at[d - 1], gz_recv.at[d - 1], tp=2 * ((z + d) % 8) + xh
        )

    for d in range(1, 8):
        gap_ring(d).start()
    for d in range(1, 8):
        gap_ring(d).wait_recv()
    total = gap_z[0]
    for n in range(1, 8):
        total = total + gap_z[n]
    gap_out[...] = total

    for d in (1, 2, 3):
        gap_far(d).wait_send()
    for d in range(1, 8):
        gap_ring(d).wait_send()
    for copy in sent:
        copy.wait_send()
    stats.wait_send()
    for copy in parts:
        copy.wait_send()


def finish(o, lse, wo_own, wo_far, value_head):
    dma = pltpu.SemaphoreType.DMA
    anywhere = pl.BlockSpec(memory_space=pl.ANY)
    vmem = pl.BlockSpec(memory_space=pltpu.VMEM)
    return pl.pallas_call(
        finish_kernel,
        out_shape=(jax.ShapeDtypeStruct((256, 512), BF), jax.ShapeDtypeStruct((8, 256), F32)),
        in_specs=[vmem, vmem, anywhere, anywhere, vmem],
        out_specs=(vmem, vmem),
        scratch_shapes=[
            pltpu.VMEM((2048, 128), BF),
            pltpu.VMEM((8, 2, 128), F32),
            pltpu.VMEM((8, 512, 512), BF),
            pltpu.VMEM((8, 512, 512), BF),
            pltpu.VMEM((2048, 128), F32),
            pltpu.VMEM((2, 256, 512), BF),
            pltpu.VMEM((4, 4, 128, 512), BF),
            pltpu.VMEM((4, 4, 128, 512), BF),
            pltpu.VMEM((8, 256), F32),
            pltpu.VMEM((4, 8, 256), F32),
            pltpu.VMEM((8, 8, 256), F32),
            dma((4,)), dma((4,)), dma((1,)), dma((1,)), dma((1,)),
            dma((4,)), dma((4,)), dma((4,)), dma((4,)), dma((1,)),
            dma((4, 4)), dma((4, 4)), dma((3,)), dma((3,)), dma((7,)), dma((7,)),
        ],
        compiler_params=pltpu.CompilerParams(
            collective_id=1, has_side_effects=True, vmem_limit_bytes=40 * MIB
        ),
        name="finish",
    )(o, lse, wo_own, wo_far, value_head)


def local(layer_in, q_weight, kv_weight, o_weight, kv_cache, cache_lengths, value_head):
    xh = lax.axis_index("tp") % 2
    x = layer_in[0].reshape(256, 512)
    qkv, wo_own, wo_far = project(x, q_weight[0], kv_weight[0], o_weight[0])
    spans = jnp.repeat(cache_lengths - xh * 256, 32).reshape(8, 2, 128)
    o, lse = attend(qkv, kv_cache[0], spans)
    hidden, gap = finish(o, lse, wo_own, wo_far, value_head.reshape(1, 512))
    hidden_out = hidden.reshape(1, 64, 4, 512)
    own_gap = lax.dynamic_slice_in_dim(gap[0].reshape(64, 4), 2 * lax.axis_index("sec"), 2, 1)
    return hidden_out, own_gap


def solution(mesh):
    placed = (
        P("sec", "grp", None, "tp"),
        P("sec", "grp", "tp"),
        P("sec", "grp", "tp"),
        P("sec", "tp", "grp"),
        P("sec", "grp", "tp", None),
        P("grp"),
        P("tp"),
    )
    return jax.shard_map(
        local,
        mesh=mesh,
        in_specs=placed,
        out_specs=(P("sec", "grp", None, "tp"), P("grp", "sec")),
        check_vma=False,
    )
```

time: 564 us -> 159 us (0.28)
  waiting for transfers between devices: 419 us -> 0 us
  Pallas kernels: 0 us -> 148 us
  blocking collectives: 73.6 us -> 0 us
  matrix products: 26.7 us -> 0 us
  between operations: 14 us -> 0.73 us
  starting transfers between devices: 9.26 us -> 0 us
  local copies, waits for them, and re-layouts: 16.1 us -> 9.67 us
    reduce_scatter x1 -> x0, waiting for transfers between devices: 214 us -> none  [local(): lax.psum_scatter(head_terms.astype(jnp.bfloat16), 'tp', scatter_dimension...]
    all_gather x4 -> x0, waiting for transfers between devices: 190 us -> none  [the longest x1 110 us: local(): full_in = lax.all_gather(local_in, 'tp', axis=1, tiled=True)]
    pallas_call x0 -> x3, Pallas kernels: none -> 148 us  [the longest x1 74.1 us: project(): pl.pallas_call(project_kernel, out_shape=(jax.ShapeDtypeStruct((2, 256, 6...]
    psum x1 -> x0, blocking collectives: 73.6 us -> none  [local(): token_gap = lax.psum(local_gap, 'tp')]
    dot_general x7 -> x0, matrix products: 26.7 us -> none  [the longest x2 11.1 us: add_rows(): return jnp.dot(full_in, piece, preferred_element_type=jnp.float32)]
    ppermute x6 -> x0, waiting for transfers between devices: 12.6 us -> none  [from_partner(): return lax.ppermute(value, axis, pairs)]
    ppermute x6 -> x0, starting transfers between devices: 9.07 us -> none  [from_partner(): return lax.ppermute(value, axis, pairs)]
    unnamed x9 -> x11, local copies, waits for them, and re-layouts: 12.4 us -> 7.42 us
  transfers between devices with their start and end apart: 11 -> 0, of which waited for: 8 -> 0; matrix products, arithmetic and copies ran while one was open for 7% -> 0% of each run, Pallas kernels for 0% -> 0%
where the time goes in v1:
time: 159 us
  Pallas kernels  148 us (93%)
  local copies, waits for them, and re-layouts  9.67 us (6%)
    pallas_call x1, Pallas kernels, project(): pl.pallas_call(project_kernel, out_shape=(jax.ShapeDtypeStruct((2, 256, 6...  74.1 us
    pallas_call x1, Pallas kernels, finish(): pl.pallas_call(finish_kernel, out_shape=(jax.ShapeDtypeStruct((256, 512),...  65.4 us
    pallas_call x1, Pallas kernels, attend(): pl.pallas_call(attend_kernel, grid=(8,), out_shape=(jax.ShapeDtypeStruct(...  8.39 us
    unnamed x11, local copies, waits for them, and re-layouts  7.42 us

profile of v1, /device:TPU:8, one launch (start us, length us, event | category | flops | bytes accessed | tf_op | source)
XLA Modules:
  0.0 159.0 jit_solution(7315255865976101412)
XLA Ops:
  0.6 0.0 copy-start.4
  0.7 0.7 broadcast_subtract_fusion
  1.3 0.1 broadcast_in_dim.7
  1.4 0.1 broadcast_in_dim.8
  1.5 0.1 broadcast_in_dim.9.len_ref
  1.6 1.0 reshape_squeeze.6.x_hbm
  2.6 0.0 copy-start.1
  2.6 1.2 copy-done.1
  3.8 0.0 copy-start.2
  3.8 1.2 copy-done.2
  5.1 0.0 copy-start.3
  5.1 0.9 copy-done.3
  6.0 74.1 %project.1 = (bf16[2,256,640]{2,1,0:T(8,128)(2,1)S(1)}, bf16[8,512,512]{2,1,0:T(8,128)(2,1)S(1)}, bf16[512,512]{1,0:T(8,128)(2,1)S(1)}) custom-call(bf16[256,512]{1,0:T(8,128)(2,1)S(1)} %reshape_squeeze.6.x_hbm, bf16[1024,512]{1,0:T(8,128)(2,1)S(1)} %bitcast.6, bf16[1024,128]{1,0:T(8,128)(2,1)S(1)} %bitcast.8, bf16[512,1024]{1,0:T(8,128)(2,1)S(1)} %bitcast.7), custom_call_target="tpu_custom_call" | custom-call | tf_op jit(solution)/shard_map/project/pallas_call | solution.py:314
  80.2 0.0 copy-start
  80.2 3.4 %copy-done = bf16[1,64,256,256]{3,2,1,0:T(8,128)(2,1)S(1)} copy-done((bf16[1,64,256,256]{3,2,1,0:T(8,128)(2,1)S(1)}, bf16[1,64,256,256]{3,2,1,0:T(8,128)(2,1)}, u32[]{:S(2)}) %copy-start) | copy-done | bytes 8388632
  83.6 8.4 %attend.1 = (bf16[2048,128]{1,0:T(8,128)(2,1)S(1)}, f32[8,2,128]{2,1,0:T(2,128)S(1)}) custom-call(bf16[2,256,640]{2,1,0:T(8,128)(2,1)S(1)} %get-tuple-element.9.q_ref, bf16[64,256,256]{2,1,0:T(8,128)(2,1)S(1)} %bitcast.5, s32[8,2,128]{2,1,0:T(2,128)S(1)} %broadcast_in_dim.9.len_ref), custom_call_target="tpu_custom_call" | custom-call | tf_op jit(solution)/shard_map/attend/pallas_call | solution.py:386
  92.0 0.0 copy-done.4
  92.0 65.4 %finish.1 = (bf16[256,512]{1,0:T(8,128)(2,1)S(1)}, f32[8,256]{1,0:T(8,128)S(1)}) custom-call(bf16[2048,128]{1,0:T(8,128)(2,1)S(1)} %get-tuple-element.10.o_ref, f32[8,2,128]{2,1,0:T(2,128)S(1)} %get-tuple-element.11.lse_ref, bf16[8,512,512]{2,1,0:T(8,128)(2,1)S(1)} %get-tuple-element.12.wo_own_hbm, bf16[512,512]{1,0:T(8,128)(2,1)S(1)} %get-tuple-element.13.wo_far_hbm, ...), custom_call_target="tpu_custom_call" | custom-call | tf_op jit(solution)/shard_map/finish/pallas_call | solution.py:558
  157.4 0.8 reshape.13
  158.2 0.1 reshape_squeeze.7
  158.3 0.1 constant_dynamic-slice_fusion
  158.3 0.6 copy.10
  (1 shorter events, 0.0 us)
Async XLA Ops:
  0.6 91.3 %copy-start.4 = (f32[512]{0:T(512)S(1)}, f32[512]{0:T(512)}, u32[]{:S(2)}) copy-start(f32[512]{0:T(512)} %param.13) | copy-start | bytes 6148
  2.6 1.2 copy-start.1
  3.8 1.2 copy-start.2
  5.1 0.9 copy-start.3
  80.2 3.4 %copy-start = (bf16[1,64,256,256]{3,2,1,0:T(8,128)(2,1)S(1)}, bf16[1,64,256,256]{3,2,1,0:T(8,128)(2,1)}, u32[]{:S(2)}) copy-start(bf16[1,64,256,256]{3,2,1,0:T(8,128)(2,1)} %param.11) | copy-start | bytes 25165828

commit v2 on v1

--- a/solution.py
+++ b/solution.py
@@ -99,10 +99,10 @@
 
 def project_kernel(
     x_hbm, wq_hbm, wkv_hbm, wo_hbm, qkv_out, wo_own, wo_far,
-    xs, ws, mine, keep, to_core, from_core, to_y, from_y, final,
+    swapped, xs, ws, mine, keep, to_core, from_core, to_y, from_y, final,
     perm_send, perm_recv, r_send, r_recv, l_send, l_recv, w_local, w_send, w_recv,
     c_send, c_recv, y_send, y_recv, a_send, a_recv, b_send, b_recv, own_sem,
-    g_send, g_recv, h_send, h_recv, g_own, f_send, f_recv,
+    g_send, g_recv, h_send, h_recv, g_own, f_send, f_recv, i_send, i_recv, j_send, j_recv, i_own,
 ):
     grp, tp, y, c, z, xh = places()
     ring_r, ring_l = 2 * ((z + 1) % 8) + xh, 2 * ((z + 7) % 8) + xh
@@ -153,12 +153,16 @@
         pltpu.make_async_copy(wq_hbm, ws.at[0, :, pl.ds(0, 512)], w_local.at[0]),
         pltpu.make_async_copy(wkv_hbm, ws.at[0, :, pl.ds(512, 128)], w_local.at[1]),
     ]
+    far_cols = pl.ds(pl.multiple_of(512 * (xh ^ 1), 512), 512)
+    far = remote(wo_hbm.at[:, far_cols], swapped, f_send.at[0], f_recv.at[0], tp=tp ^ 1)
+    far.start()
     for copy in w_out + w_in:
         copy.start()
     wo = OutputWeights(
         wo_hbm.at[:, pl.ds(pl.multiple_of(512 * xh, 512), 512)], wo_own, g_send, g_recv, h_send, h_recv, g_own.at[0]
     )
     wo.start()
+    wo2 = OutputWeights(swapped, wo_far, i_send, i_recv, j_send, j_recv, i_own.at[0])
 
     def ring(right, k, ch, place):
         ss, rs, to = (r_send, r_recv, ring_r) if right else (l_send, l_recv, ring_l)
@@ -234,23 +238,32 @@
                 ring(right, k, ch, place).wait_recv()
                 if k < 4 and travels(right, k + 1, ch):
                     send(ring(right, k + 1, ch, place))
-        compute(0, k - 1)
-        if k > 1:
-            pass_on(0, k - 2)
+        if k < 4:
+            compute(0, k - 1)
+        if k == 1:
+            far.wait_recv()
+            wo2.start()
         if k == 2:
+            pass_on(0, 0)
             wo.middle()
+        if k == 3:
+            pass_on(0, 1)
+            for copy in w_out:
+                copy.wait_recv()
+            compute(1, 0)
+            compute(1, 1)
+            pass_on(0, 2)
+            compute(1, 2)
+            wo.last()
+            wo2.middle()
+            pass_on(1, 0)
+            pass_on(1, 1)
+    compute(0, 3)
+    compute(1, 3)
+    pass_on(1, 2)
     pass_on(0, 3)
-    for copy in w_out:
-        copy.wait_recv()
-    far_cols = pl.ds(pl.multiple_of(512 * (xh ^ 1), 512), 512)
-    far = remote(wo_hbm.at[:, far_cols], wo_far, f_send.at[0], f_recv.at[0], tp=tp ^ 1)
-    far.start()
-    for i in range(4):
-        compute(1, i)
-        if i > 0:
-            pass_on(1, i - 1)
     pass_on(1, 3)
-    wo.last()
+    wo2.last()
 
     near = c == xh
 
@@ -305,7 +318,8 @@
             d = (order[i] - y + 4) % 4
             pl.when(d != 0)(lambda j=j, i=i, d=d: y_copy(j, i, d).wait_send())
     wo.finish()
-    far.wait()
+    wo2.finish()
+    far.wait_send()
 
 
 def project(x, wq, wkv, wo):
@@ -316,11 +330,12 @@
         out_shape=(
             jax.ShapeDtypeStruct((2, 256, 640), BF),
             jax.ShapeDtypeStruct((8, 512, 512), BF),
-            jax.ShapeDtypeStruct((512, 512), BF),
+            jax.ShapeDtypeStruct((8, 512, 512), BF),
         ),
         in_specs=[anywhere] * 4,
         out_specs=(anywhere,) * 3,
         scratch_shapes=[
+            pltpu.VMEM((512, 512), BF),
             pltpu.VMEM((8, 256, 512), BF),
             pltpu.VMEM((2, 1024, 640), BF),
             pltpu.VMEM((2, 4, 128, 640), F32),
@@ -333,9 +348,10 @@
             dma((2,)), dma((2,)), dma((4, 2)), dma((4, 2)), dma((4, 2)), dma((4, 2)), dma((2,)), dma((2,)), dma((2,)),
             dma((2, 4)), dma((2, 4)), dma((2, 4)), dma((2, 3)), dma((2,)), dma((2,)), dma((2,)), dma((2, 2)), dma((2,)),
             dma((4,)), dma((4,)), dma((4,)), dma((4,)), dma((1,)), dma((1,)), dma((1,)),
+            dma((4,)), dma((4,)), dma((4,)), dma((4,)), dma((1,)),
         ],
         compiler_params=pltpu.CompilerParams(
-            collective_id=0, has_side_effects=True, vmem_limit_bytes=40 * MIB
+            collective_id=0, has_side_effects=True, vmem_limit_bytes=58 * MIB
         ),
         name="project",
     )(x, wq, wkv, wo)
@@ -397,7 +413,7 @@
             pl.BlockSpec((1, 2, 128), lambda i: (i, 0, 0)),
         ),
         scratch_shapes=[pltpu.VMEM((128, 128), F32)],
-        compiler_params=pltpu.CompilerParams(vmem_limit_bytes=16 * MIB),
+        compiler_params=pltpu.CompilerParams(vmem_limit_bytes=58 * MIB),
         name="attend",
     )(qkv, cache, spans)
 
@@ -406,7 +422,6 @@
     o_ref, lse_ref, wo_own_hbm, wo_far_hbm, head_ref, hidden_out, gap_out,
     o_got, lse_got, near_w, far_w, merged, ctx, outgo, income, gap_own, gap_x, gap_z,
     o_send, o_recv, s_send, s_recv, near_sem,
-    g_send, g_recv, h_send, h_recv, g_own,
     ring_send, ring_recv, gx_send, gx_recv, gz_send, gz_recv,
 ):
     grp, tp, y, c, z, xh = places()
@@ -419,12 +434,9 @@
     greet(tp=tp ^ 1)
     greet(sec=sec ^ 1)
     greet(tp=tp ^ 1, sec=sec ^ 1)
-    greet(grp=grp ^ 1)
-    for d in (1, 2, 3):
-        greet(grp=2 * ((y + d) % 4) + c)
     for d in range(1, 8):
         greet(tp=2 * ((z + d) % 8) + xh)
-    pl.semaphore_wait(barrier, 14)
+    pl.semaphore_wait(barrier, 10)
 
     stats = remote(lse_ref, lse_got, s_send.at[0], s_recv.at[0], tp=tp ^ 1)
     stats.start()
@@ -435,8 +447,8 @@
         parts[-1].start()
     near = pltpu.make_async_copy(wo_own_hbm, near_w, near_sem.at[0])
     near.start()
-    wo = OutputWeights(wo_far_hbm, far_w, g_send, g_recv, h_send, h_recv, g_own.at[0])
-    wo.start()
+    other = pltpu.make_async_copy(wo_far_hbm, far_w, near_sem.at[1])
+    other.start()
 
     stats.wait_recv()
     for n in range(4):
@@ -448,14 +460,11 @@
             own = o_ref[block, :].astype(F32)
             got = o_got[block, :].astype(F32)
             merged[block, :] = own * factor + got * (1.0 - factor)
-        if n == 1:
-            wo.middle()
     for part in (0, 1):
         for head in range(4):
             ctx[part, :, pl.ds(128 * head, 128)] = merged[pl.ds(4 * part + head, 256, stride=8), :].astype(BF)
     near.wait()
-    wo.last()
-    wo.finish()
+    other.wait()
 
     def block(place, ch):
         return dot(ctx[xh, 128 * ch:128 * ch + 128, :], near_w[place]) + dot(
@@ -572,12 +581,11 @@
             pltpu.VMEM((8, 256), F32),
             pltpu.VMEM((4, 8, 256), F32),
             pltpu.VMEM((8, 8, 256), F32),
-            dma((4,)), dma((4,)), dma((1,)), dma((1,)), dma((1,)),
-            dma((4,)), dma((4,)), dma((4,)), dma((4,)), dma((1,)),
+            dma((4,)), dma((4,)), dma((1,)), dma((1,)), dma((2,)),
             dma((4, 4)), dma((4, 4)), dma((3,)), dma((3,)), dma((7,)), dma((7,)),
         ],
         compiler_params=pltpu.CompilerParams(
-            collective_id=1, has_side_effects=True, vmem_limit_bytes=40 * MIB
+            collective_id=1, has_side_effects=True, vmem_limit_bytes=58 * MIB
         ),
         name="finish",
     )(o, lse, wo_own, wo_far, value_head)

time: 159 us -> 168 us (1.057); the launches traced: 159 us -> 166 us
  Pallas kernels: 148 us -> 159 us
  local copies, waits for them, and re-layouts: 9.67 us -> 5.84 us
    unnamed x11 -> x1, local copies, waits for them, and re-layouts: 7.42 us -> 0.64 us
    pallas_call x1, Pallas kernels: 74.1 us -> 78.4 us  [project(): pl.pallas_call(project_kernel, out_shape=(jax.ShapeDtypeStruct((2, 256, 6...]
    pallas_call x1, Pallas kernels: 65.4 us -> 69.3 us  [finish(): pl.pallas_call(finish_kernel, out_shape=(jax.ShapeDtypeStruct((256, 512),...]
    pallas_call x1, Pallas kernels: 8.39 us -> 11.1 us  [attend(): pl.pallas_call(attend_kernel, grid=(8,), out_shape=(jax.ShapeDtypeStruct(...]
where the time goes in v2:
time: 168 us; the launch traced here: 166 us
  Pallas kernels  159 us (95%)
  local copies, waits for them, and re-layouts  5.84 us (3%)
    pallas_call x1, Pallas kernels, project(): pl.pallas_call(project_kernel, out_shape=(jax.ShapeDtypeStruct((2, 256, 6...  78.4 us
    pallas_call x1, Pallas kernels, finish(): pl.pallas_call(finish_kernel, out_shape=(jax.ShapeDtypeStruct((256, 512),...  69.3 us
    pallas_call x1, Pallas kernels, attend(): pl.pallas_call(attend_kernel, grid=(8,), out_shape=(jax.ShapeDtypeStruct(...  11.1 us

profile of v2, /device:TPU:8, one launch (start us, length us, event | category | flops | bytes accessed | tf_op | source)
XLA Modules:
  0.0 166.0 jit_solution(17616015599266167342)
XLA Ops:
  0.6 0.7 broadcast_subtract_fusion
  1.3 0.1 broadcast_in_dim.7
  1.4 0.1 broadcast_in_dim.8
  1.5 0.7 broadcast_in_dim.9.len_ref
  2.2 1.7 %reshape_squeeze.6.x_hbm = bf16[256,512]{1,0:T(8,128)(2,1)} reshape(bf16[1,64,4,512]{3,2,1,0:T(4,128)(2,1)} %param.7) | data formatting | bytes 524288 | tf_op jit(solution)/shard_map/reshape;squeeze | solution.py:596
  3.9 78.4 %project.1 = (bf16[2,256,640]{2,1,0:T(8,128)(2,1)}, bf16[8,512,512]{2,1,0:T(8,128)(2,1)}, bf16[8,512,512]{2,1,0:T(8,128)(2,1)}) custom-call(bf16[256,512]{1,0:T(8,128)(2,1)} %reshape_squeeze.6.x_hbm, bf16[1024,512]{1,0:T(8,128)(2,1)} %bitcast.6, bf16[1024,128]{1,0:T(8,128)(2,1)} %bitcast.8, bf16[512,1024]{1,0:T(8,128)(2,1)} %bitcast.7), custom_call_target="tpu_custom_call" | custom-call | tf_op jit(solution)/shard_map/project/pallas_call | solution.py:328
  82.3 11.1 %attend.1 = (bf16[2048,128]{1,0:T(8,128)(2,1)}, f32[8,2,128]{2,1,0:T(2,128)}) custom-call(bf16[2,256,640]{2,1,0:T(8,128)(2,1)} %get-tuple-element.9.q_ref, bf16[64,256,256]{2,1,0:T(8,128)(2,1)} %bitcast.5, s32[8,2,128]{2,1,0:T(2,128)} %broadcast_in_dim.9.len_ref), custom_call_target="tpu_custom_call" | custom-call | tf_op jit(solution)/shard_map/attend/pallas_call | solution.py:402
  93.4 69.3 %finish.1 = (bf16[256,512]{1,0:T(8,128)(2,1)}, f32[8,256]{1,0:T(8,128)}) custom-call(bf16[2048,128]{1,0:T(8,128)(2,1)} %get-tuple-element.10.o_ref, f32[8,2,128]{2,1,0:T(2,128)} %get-tuple-element.11.lse_ref, bf16[8,512,512]{2,1,0:T(8,128)(2,1)} %get-tuple-element.12.wo_own_hbm, bf16[8,512,512]{2,1,0:T(8,128)(2,1)} %get-tuple-element.13.wo_far_hbm, ...), custom_call_target="tpu_custom_call" | custom-call | tf_op jit(solution)/shard_map/finish/pallas_call | solution.py:567
  162.7 1.7 %reshape.13 = bf16[1,64,4,512]{3,2,1,0:T(4,128)(2,1)} reshape(bf16[256,512]{1,0:T(8,128)(2,1)} %get-tuple-element.14) | data formatting | bytes 524288 | tf_op jit(solution)/shard_map/reshape | solution.py:601
  164.4 0.7 slice_reduce_fusion
  165.1 0.1 reshape_squeeze.7
  165.2 0.1 constant_dynamic-slice_fusion
  165.3 0.6 copy.10

commit v3 on v1

--- a/solution.py
+++ b/solution.py
@@ -335,124 +335,124 @@
             dma((4,)), dma((4,)), dma((4,)), dma((4,)), dma((1,)), dma((1,)), dma((1,)),
         ],
         compiler_params=pltpu.CompilerParams(
-            collective_id=0, has_side_effects=True, vmem_limit_bytes=40 * MIB
+            collective_id=0, has_side_effects=True, vmem_limit_bytes=58 * MIB
         ),
         name="project",
     )(x, wq, wkv, wo)
 
 
-def attend_kernel(q_ref, kv_ref, len_ref, out_ref, lse_ref, q_rows):
-    step = pl.program_id(0)
-    leader = lax.axis_index("tp") % 2 == 0
+def attend(group, q_ref, kv_ref, len_ref, out_ref, lse_ref, q_rows, leader):
     scale = HD ** -0.5
     lane = lax.broadcasted_iota(jnp.int32, (1, 128), 1)
     pos = lax.broadcasted_iota(jnp.int32, (256, 128), 0)
     lane_roll, lane_step = lane // 32, lane % 32 // 8
     new_row = lax.broadcasted_iota(jnp.int32, (16, 128), 0)
     causal = (new_row // 4 == lane_roll) & (new_row % 4 <= lane_step) & leader
-    for group in range(2):
-        tokens = pl.ds(16 * group, 16)
-        for part in (0, 1):
-            vals = q_ref[part, tokens, :].astype(F32)
-            for head in range(4):
-                q_rows[pl.ds(4 * part + head, 16, stride=8), :] = vals[:, 128 * head:128 * head + 128]
-        new_key = q_ref[0, tokens, 512:]
-        new_val = q_ref[1, tokens, 512:]
-        q_t = q_rows[...].T.astype(BF)
-        cached = None
-        for i in range(4):
-            one = dot(kv_ref[4 * group + i, :, :128], q_t)
-            cached = one if cached is None else jnp.where(lane_roll == i, one, cached)
-        visible = pos < len_ref[0, group:group + 1, :]
-        cached = jnp.where(visible, cached * scale, -1e30)
-        fresh = jnp.where(causal, dot(new_key, q_t) * scale, -1e30)
-        peak = jnp.maximum(jnp.max(cached, axis=0, keepdims=True), jnp.max(fresh, axis=0, keepdims=True))
-        cached = jnp.where(visible, jnp.exp(cached - peak), 0.0)
-        fresh = jnp.where(causal, jnp.exp(fresh - peak), 0.0)
-        total = jnp.sum(cached, axis=0, keepdims=True) + jnp.sum(fresh, axis=0, keepdims=True)
-        lse_ref[0, group:group + 1, :] = jnp.where(total > 0.0, peak + jnp.log(jnp.maximum(total, 1e-30)), -1e30)
-        inverse = jnp.where(total > 0.0, 1.0 / jnp.maximum(total, 1e-30), 0.0)
-        weights = (cached * inverse).T.astype(BF)
-        fresh_w = jnp.concatenate([fresh * inverse, jnp.zeros((112, 128), F32)], axis=0).T.astype(BF)
-        new_pad = jnp.concatenate([new_val, jnp.zeros((112, 128), BF)], axis=0)
-        added = dot(fresh_w, new_pad)
-        for i in range(4):
-            block = slice(32 * i, 32 * i + 32)
-            got = dot(weights[block], kv_ref[4 * group + i, :, 128:]) + added[block]
-            out_ref[pl.ds(128 * group + 32 * i, 32), :] = got.astype(BF)
-
-
-def attend(qkv, cache, spans):
-    return pl.pallas_call(
-        attend_kernel,
-        grid=(8,),
-        out_shape=(jax.ShapeDtypeStruct((2048, 128), BF), jax.ShapeDtypeStruct((8, 2, 128), F32)),
-        in_specs=[
-            pl.BlockSpec((2, 32, 640), lambda i: (0, i, 0)),
-            pl.BlockSpec((8, 256, 256), lambda i: (i, 0, 0)),
-            pl.BlockSpec((1, 2, 128), lambda i: (i, 0, 0)),
-        ],
-        out_specs=(
-            pl.BlockSpec((256, 128), lambda i: (i, 0)),
-            pl.BlockSpec((1, 2, 128), lambda i: (i, 0, 0)),
-        ),
-        scratch_shapes=[pltpu.VMEM((128, 128), F32)],
-        compiler_params=pltpu.CompilerParams(vmem_limit_bytes=16 * MIB),
-        name="attend",
-    )(qkv, cache, spans)
+    tokens = pl.ds(pl.multiple_of(16 * group, 16), 16)
+    for part in (0, 1):
+        vals = q_ref[part, tokens, :].astype(F32)
+        for head in range(4):
+            q_rows[pl.ds(4 * part + head, 16, stride=8), :] = vals[:, 128 * head:128 * head + 128]
+    new_key = q_ref[0, tokens, 512:]
+    new_val = q_ref[1, tokens, 512:]
+    q_t = q_rows[...].T.astype(BF)
+    cached = None
+    for i in range(4):
+        one = dot(kv_ref[4 * group + i, :, :128], q_t)
+        cached = one if cached is None else jnp.where(lane_roll == i, one, cached)
+    visible = pos < len_ref[group]
+    cached = jnp.where(visible, cached * scale, -1e30)
+    fresh = jnp.where(causal, dot(new_key, q_t) * scale, -1e30)
+    peak = jnp.maximum(jnp.max(cached, axis=0, keepdims=True), jnp.max(fresh, axis=0, keepdims=True))
+    cached = jnp.where(visible, jnp.exp(cached - peak), 0.0)
+    fresh = jnp.where(causal, jnp.exp(fresh - peak), 0.0)
+    total = jnp.sum(cached, axis=0, keepdims=True) + jnp.sum(fresh, axis=0, keepdims=True)
+    lse_ref[group] = jnp.where(total > 0.0, peak + jnp.log(jnp.maximum(total, 1e-30)), -1e30)
+    inverse = jnp.where(total > 0.0, 1.0 / jnp.maximum(total, 1e-30), 0.0)
+    weights = (cached * inverse).T.astype(BF)
+    fresh_w = jnp.concatenate([fresh * inverse, jnp.zeros((112, 128), F32)], axis=0).T.astype(BF)
+    new_pad = jnp.concatenate([new_val, jnp.zeros((112, 128), BF)], axis=0)
+    added = dot(fresh_w, new_pad)
+    for i in range(4):
+        block = slice(32 * i, 32 * i + 32)
+        got = dot(weights[block], kv_ref[4 * group + i, :, 128:]) + added[block]
+        out_ref[pl.ds(pl.multiple_of(128 * group + 32 * i, 32), 32), :] = got.astype(BF)
 
 
 def finish_kernel(
-    o_ref, lse_ref, wo_own_hbm, wo_far_hbm, head_ref, hidden_out, gap_out,
-    o_got, lse_got, near_w, far_w, merged, ctx, outgo, income, gap_own, gap_x, gap_z,
-    o_send, o_recv, s_send, s_recv, near_sem,
+    q_ref, kv_hbm, len_ref, wo_own_hbm, wo_far_hbm, head_ref, hidden_out, gap_out,
+    kv, q_rows, o_own, lse_own, o_got, lse_got, near_w, far_w, merged, ctx, outgo, income, gap_own, gaps_all,
+    kv_sem, o_send, o_recv, s_send, s_recv, near_sem, ring_send, ring_recv, gap_send, gap_recv,
     g_send, g_recv, h_send, h_recv, g_own,
-    ring_send, ring_recv, gx_send, gx_recv, gz_send, gz_recv,
 ):
     grp, tp, y, c, z, xh = places()
     sec = lax.axis_index("sec")
     barrier = pltpu.get_barrier_semaphore()
 
-    def greet(**where):
+    def others():
+        for d in range(1, 32):
+            yield d - 1, dict(tp=(tp + d % 16) % 16, sec=sec ^ (d // 16))
+
+    for _, where in others():
         pl.semaphore_signal(barrier, inc=1, device_id=where, device_id_type=MESH)
-
-    greet(tp=tp ^ 1)
-    greet(sec=sec ^ 1)
-    greet(tp=tp ^ 1, sec=sec ^ 1)
-    greet(grp=grp ^ 1)
-    for d in (1, 2, 3):
-        greet(grp=2 * ((y + d) % 4) + c)
-    for d in range(1, 8):
-        greet(tp=2 * ((z + d) % 8) + xh)
-    pl.semaphore_wait(barrier, 14)
-
-    stats = remote(lse_ref, lse_got, s_send.at[0], s_recv.at[0], tp=tp ^ 1)
-    stats.start()
-    parts = []
-    for n in range(4):
-        block = pl.ds(512 * n, 512)
-        parts.append(remote(o_ref.at[block], o_got.at[block], o_send.at[n], o_recv.at[n], tp=tp ^ 1))
-        parts[-1].start()
+    for away in (grp ^ 1, 2 * ((y + 1) % 4) + c, 2 * ((y + 3) % 4) + c):
+        pl.semaphore_signal(barrier, inc=1, device_id={"grp": away}, device_id_type=MESH)
+
+    def cache_copy(n):
+        rollouts = pl.ds(pl.multiple_of(8 * n, 8), 8)
+        return pltpu.make_async_copy(kv_hbm.at[rollouts], kv.at[rollouts], kv_sem.at[n])
+
+    for n in range(8):
+        cache_copy(n).start()
     near = pltpu.make_async_copy(wo_own_hbm, near_w, near_sem.at[0])
     near.start()
     wo = OutputWeights(wo_far_hbm, far_w, g_send, g_recv, h_send, h_recv, g_own.at[0])
+    pl.semaphore_wait(barrier, 34)
     wo.start()
 
-    stats.wait_recv()
-    for n in range(4):
-        parts[n].wait_recv()
+    def attend_part(n):
+        def body(m, carry):
+            cache_copy(m).wait()
+            for lane in (0, 1):
+                attend(2 * m + lane, q_ref, kv, len_ref, o_own, lse_own, q_rows.at[lane], xh == 0)
+            return carry
+
+        lax.fori_loop(2 * n, 2 * n + 2, body, 0)
+
+    def o_copy(n):
+        block = pl.ds(512 * n, 512)
+        return remote(o_own.at[block], o_got.at[block], o_send.at[n], o_recv.at[n], tp=tp ^ 1)
+
+    def lse_copy(n):
+        block = pl.ds(4 * n, 4)
+        return remote(lse_own.at[block], lse_got.at[block], s_send.at[n], s_recv.at[n], tp=tp ^ 1)
+
+    def merge(n):
+        lse_copy(n).wait_recv()
+        o_copy(n).wait_recv()
         for m in range(4 * n, 4 * n + 4):
-            factor = 1.0 / (1.0 + jnp.exp(lse_got[m // 2, m % 2:m % 2 + 1, :] - lse_ref[m // 2, m % 2:m % 2 + 1, :]))
+            factor = 1.0 / (1.0 + jnp.exp(lse_got[m] - lse_own[m]))
             factor = jnp.broadcast_to(factor, (128, 128)).T
             block = slice(128 * m, 128 * m + 128)
-            own = o_ref[block, :].astype(F32)
+            own = o_own[block, :].astype(F32)
             got = o_got[block, :].astype(F32)
             merged[block, :] = own * factor + got * (1.0 - factor)
-        if n == 1:
+        for part in (0, 1):
+            for head in range(4):
+                ctx[part, pl.ds(64 * n, 64), pl.ds(128 * head, 128)] = merged[
+                    pl.ds(512 * n + 4 * part + head, 64, stride=8), :
+                ].astype(BF)
+
+    for n in range(4):
+        attend_part(n)
+        lse_copy(n).start()
+        o_copy(n).start()
+        if n > 1:
+            merge(n - 2)
+        if n == 3:
             wo.middle()
-    for part in (0, 1):
-        for head in range(4):
-            ctx[part, :, pl.ds(128 * head, 128)] = merged[pl.ds(4 * part + head, 256, stride=8), :].astype(BF)
+    merge(2)
+    merge(3)
     near.wait()
     wo.last()
     wo.finish()
@@ -509,89 +509,76 @@
         result = total.astype(BF)
         hidden_out[128 * ch:128 * ch + 128, :] = result
         gaps.append(jnp.sum(dot_nt(triple, result), axis=0, keepdims=True))
-    gap = jnp.concatenate(gaps, axis=1)
+    gap = jnp.concatenate(gaps + [jnp.zeros((6, 128), F32)], axis=0)
     gap = jnp.where(sec == 0, gap, -gap)
-    own_x = 2 * xh + sec
-    gap_own[...] = jnp.broadcast_to(gap, (8, 256))
-
-    def gap_far(d):
-        return remote(
-            gap_own, gap_x.at[own_x], gx_send.at[d - 1], gx_recv.at[d - 1], tp=tp ^ (d // 2), sec=sec ^ (d % 2)
-        )
-
-    for d in (1, 2, 3):
-        gap_far(d).start()
-    gap_x[own_x] = gap_own[...]
-    for d in (1, 2, 3):
-        gap_far(d).wait_recv()
-    gap_z[z] = gap_x[0] + gap_x[1] + gap_x[2] + gap_x[3]
-
-    def gap_ring(d):
-        return remote(
-            gap_z.at[z], gap_z.at[z], gz_send.at[d - 1], gz_recv.at[d - 1], tp=2 * ((z + d) % 8) + xh
-        )
-
-    for d in range(1, 8):
-        gap_ring(d).start()
-    for d in range(1, 8):
-        gap_ring(d).wait_recv()
-    total = gap_z[0]
-    for n in range(1, 8):
-        total = total + gap_z[n]
+    own_place = 16 * sec + tp
+    gap_own[...] = gap
+    gaps_all[own_place] = gap
+
+    def gap_copy(n, where):
+        return remote(gap_own, gaps_all.at[own_place], gap_send.at[n], gap_recv.at[n], **where)
+
+    for n, where in others():
+        gap_copy(n, where).start()
+    for n, where in others():
+        gap_copy(n, where).wait_recv()
+    total = gaps_all[0]
+    for n in range(1, 32):
+        total = total + gaps_all[n]
     gap_out[...] = total
 
-    for d in (1, 2, 3):
-        gap_far(d).wait_send()
-    for d in range(1, 8):
-        gap_ring(d).wait_send()
+    for n, where in others():
+        gap_copy(n, where).wait_send()
     for copy in sent:
         copy.wait_send()
-    stats.wait_send()
-    for copy in parts:
-        copy.wait_send()
-
-
-def finish(o, lse, wo_own, wo_far, value_head):
+    for n in range(4):
+        lse_copy(n).wait_send()
+        o_copy(n).wait_send()
+
+
+def finish(qkv, cache, spans, wo_own, wo_far, value_head):
     dma = pltpu.SemaphoreType.DMA
     anywhere = pl.BlockSpec(memory_space=pl.ANY)
     vmem = pl.BlockSpec(memory_space=pltpu.VMEM)
     return pl.pallas_call(
         finish_kernel,
-        out_shape=(jax.ShapeDtypeStruct((256, 512), BF), jax.ShapeDtypeStruct((8, 256), F32)),
-        in_specs=[vmem, vmem, anywhere, anywhere, vmem],
+        out_shape=(jax.ShapeDtypeStruct((256, 512), BF), jax.ShapeDtypeStruct((8, 128), F32)),
+        in_specs=[vmem, anywhere, vmem, anywhere, anywhere, vmem],
         out_specs=(vmem, vmem),
         scratch_shapes=[
+            pltpu.VMEM((64, 256, 256), BF),
+            pltpu.VMEM((2, 128, 128), F32),
             pltpu.VMEM((2048, 128), BF),
-            pltpu.VMEM((8, 2, 128), F32),
+            pltpu.VMEM((16, 1, 128), F32),
+            pltpu.VMEM((2048, 128), BF),
+            pltpu.VMEM((16, 1, 128), F32),
             pltpu.VMEM((8, 512, 512), BF),
             pltpu.VMEM((8, 512, 512), BF),
             pltpu.VMEM((2048, 128), F32),
             pltpu.VMEM((2, 256, 512), BF),
             pltpu.VMEM((4, 4, 128, 512), BF),
             pltpu.VMEM((4, 4, 128, 512), BF),
-            pltpu.VMEM((8, 256), F32),
-            pltpu.VMEM((4, 8, 256), F32),
-            pltpu.VMEM((8, 8, 256), F32),
-            dma((4,)), dma((4,)), dma((1,)), dma((1,)), dma((1,)),
+            pltpu.VMEM((8, 128), F32),
+            pltpu.VMEM((32, 8, 128), F32),
+            dma((8,)), dma((4,)), dma((4,)), dma((4,)), dma((4,)), dma((1,)),
+            dma((4, 4)), dma((4, 4)), dma((31,)), dma((31,)),
             dma((4,)), dma((4,)), dma((4,)), dma((4,)), dma((1,)),
-            dma((4, 4)), dma((4, 4)), dma((3,)), dma((3,)), dma((7,)), dma((7,)),
         ],
         compiler_params=pltpu.CompilerParams(
-            collective_id=1, has_side_effects=True, vmem_limit_bytes=40 * MIB
+            collective_id=1, has_side_effects=True, vmem_limit_bytes=58 * MIB
         ),
         name="finish",
-    )(o, lse, wo_own, wo_far, value_head)
+    )(qkv, cache, spans, wo_own, wo_far, value_head)
 
 
 def local(layer_in, q_weight, kv_weight, o_weight, kv_cache, cache_lengths, value_head):
     xh = lax.axis_index("tp") % 2
     x = layer_in[0].reshape(256, 512)
     qkv, wo_own, wo_far = project(x, q_weight[0], kv_weight[0], o_weight[0])
-    spans = jnp.repeat(cache_lengths - xh * 256, 32).reshape(8, 2, 128)
-    o, lse = attend(qkv, kv_cache[0], spans)
-    hidden, gap = finish(o, lse, wo_own, wo_far, value_head.reshape(1, 512))
+    spans = jnp.repeat(cache_lengths - xh * 256, 32).reshape(16, 1, 128)
+    hidden, gap = finish(qkv, kv_cache[0], spans, wo_own, wo_far, value_head.reshape(1, 512))
     hidden_out = hidden.reshape(1, 64, 4, 512)
-    own_gap = lax.dynamic_slice_in_dim(gap[0].reshape(64, 4), 2 * lax.axis_index("sec"), 2, 1)
+    own_gap = lax.dynamic_slice_in_dim(gap[:2].reshape(64, 4), 2 * lax.axis_index("sec"), 2, 1)
     return hidden_out, own_gap
 
 

time: 159 us -> 150 us (0.943)
  Pallas kernels: 148 us -> 142 us
  local copies, waits for them, and re-layouts: 9.67 us -> 5.8 us
    pallas_call x1 -> x0, Pallas kernels: 8.39 us -> none  [attend(): pl.pallas_call(attend_kernel, grid=(8,), out_shape=(jax.ShapeDtypeStruct(...]
    unnamed x11 -> x1, local copies, waits for them, and re-layouts: 7.42 us -> 0.64 us
    pallas_call x1, Pallas kernels: 65.4 us -> 67.3 us  [finish(): pl.pallas_call(finish_kernel, out_shape=(jax.ShapeDtypeStruct((256, 512),...]
where the time goes in v3:
time: 150 us; the launch traced here: 149 us
  Pallas kernels  142 us (95%)
  local copies, waits for them, and re-layouts  5.8 us (4%)
    pallas_call x1, Pallas kernels, project(): pl.pallas_call(project_kernel, out_shape=(jax.ShapeDtypeStruct((2, 256, 6...  74.4 us
    pallas_call x1, Pallas kernels, finish(): pl.pallas_call(finish_kernel, out_shape=(jax.ShapeDtypeStruct((256, 512),...  67.3 us

profile of v3, /device:TPU:8, one launch (start us, length us, event | category | flops | bytes accessed | tf_op | source)
XLA Modules:
  0.0 148.9 jit_solution(17151511760323253096)
XLA Ops:
  0.6 0.7 broadcast_subtract_fusion
  1.3 0.1 broadcast_in_dim.7
  1.4 0.1 broadcast_in_dim.8
  1.5 0.7 broadcast_in_dim.9.len_ref
  2.2 1.7 %reshape_squeeze.3.x_hbm = bf16[256,512]{1,0:T(8,128)(2,1)} reshape(bf16[1,64,4,512]{3,2,1,0:T(4,128)(2,1)} %param.7) | data formatting | bytes 524288 | tf_op jit(solution)/shard_map/reshape;squeeze | solution.py:576
  3.9 74.4 %project.1 = (bf16[2,256,640]{2,1,0:T(8,128)(2,1)}, bf16[8,512,512]{2,1,0:T(8,128)(2,1)}, bf16[512,512]{1,0:T(8,128)(2,1)}) custom-call(bf16[256,512]{1,0:T(8,128)(2,1)} %reshape_squeeze.3.x_hbm, bf16[1024,512]{1,0:T(8,128)(2,1)} %bitcast.6, bf16[1024,128]{1,0:T(8,128)(2,1)} %bitcast.8, bf16[512,1024]{1,0:T(8,128)(2,1)} %bitcast.7), custom_call_target="tpu_custom_call" | custom-call | tf_op jit(solution)/shard_map/project/pallas_call | solution.py:314
  78.3 67.3 %finish.1 = (bf16[256,512]{1,0:T(8,128)(2,1)}, f32[8,128]{1,0:T(8,128)}) custom-call(bf16[2,256,640]{2,1,0:T(8,128)(2,1)} %get-tuple-element.7.q_ref, bf16[64,256,256]{2,1,0:T(8,128)(2,1)} %bitcast.5, s32[16,1,128]{2,1,0:T(1,128)} %broadcast_in_dim.9.len_ref, bf16[8,512,512]{2,1,0:T(8,128)(2,1)} %get-tuple-element.8.wo_own_hbm, ...), custom_call_target="tpu_custom_call" | custom-call | tf_op jit(solution)/shard_map/finish/pallas_call | solution.py:543
  145.7 1.7 %reshape.21 = bf16[1,64,4,512]{3,2,1,0:T(4,128)(2,1)} reshape(bf16[256,512]{1,0:T(8,128)(2,1)} %get-tuple-element.10) | data formatting | bytes 524288 | tf_op jit(solution)/shard_map/reshape | solution.py:580
  147.4 0.7 slice.3
  148.1 0.1 reshape.22
  148.2 0.1 constant_dynamic-slice_fusion
  148.3 0.6 copy.10

commit v4 on v3

--- a/solution.py
+++ b/solution.py
@@ -97,17 +97,18 @@
             self.from_core(slot, self.grp).wait_recv()
 
 
-def project_kernel(
-    x_hbm, wq_hbm, wkv_hbm, wo_hbm, qkv_out, wo_own, wo_far,
+def project(
+    x_hbm, wq_hbm, wkv_hbm, wo_hbm, qkv_out, wo_own, swapped, wo_far, begin,
     xs, ws, mine, keep, to_core, from_core, to_y, from_y, final,
     perm_send, perm_recv, r_send, r_recv, l_send, l_recv, w_local, w_send, w_recv,
     c_send, c_recv, y_send, y_recv, a_send, a_recv, b_send, b_recv, own_sem,
-    g_send, g_recv, h_send, h_recv, g_own, f_send, f_recv,
+    g_send, g_recv, h_send, h_recv, g_own, f_send, f_recv, i_send, i_recv, j_send, j_recv, i_own,
 ):
     grp, tp, y, c, z, xh = places()
     ring_r, ring_l = 2 * ((z + 1) % 8) + xh, 2 * ((z + 7) % 8) + xh
-    dst_grp, dst_tp = z, 2 * (2 * y + xh) + c
-    src_grp, src_tp = 2 * (z // 2) + xh, 2 * grp + z % 2
+    spot = (z - 2 * y - 4 * xh + 16) % 8
+    dst_grp, dst_tp = z, 2 * ((2 * (z // 2) + 2 * y + xh + 4 * c) % 8) + c
+    src_grp, src_tp = 2 * (spot // 2) + xh, 2 * grp + spot % 2
     stays = (dst_grp == grp) & (dst_tp == tp)
     moves = jnp.logical_not(stays)
 
@@ -121,14 +122,17 @@
         greet(grp=dst_grp, tp=dst_tp)
         greet(grp=src_grp, tp=src_tp)
 
-    greet(tp=ring_r)
-    greet(tp=ring_l)
+    sec = lax.axis_index("sec")
     greet(tp=tp ^ 1)
+    greet(sec=sec ^ 1)
+    greet(tp=tp ^ 1, sec=sec ^ 1)
+    for d in range(1, 8):
+        greet(tp=2 * ((z + d) % 8) + xh)
     greet(grp=grp ^ 1)
     greet(grp=grp ^ 1, tp=tp ^ 1)
     for d in (1, 2, 3):
         greet(grp=2 * ((y + d) % 4) + c)
-    pl.semaphore_wait(barrier, jnp.where(moves, 10, 8))
+    pl.semaphore_wait(barrier, jnp.where(moves, 17, 15))
 
     def rows(ch):
         return pl.ds(128 * ch, 128)
@@ -139,7 +143,7 @@
         )
 
     def perm_local(ch):
-        return pltpu.make_async_copy(x_hbm.at[rows(ch)], xs.at[z, rows(ch)], perm_recv.at[ch])
+        return pltpu.make_async_copy(x_hbm.at[rows(ch)], xs.at[spot, rows(ch)], perm_recv.at[ch])
 
     for ch in (0, 1):
         pl.when(moves)(lambda ch=ch: perm(ch).start())
@@ -159,6 +163,8 @@
         wo_hbm.at[:, pl.ds(pl.multiple_of(512 * xh, 512), 512)], wo_own, g_send, g_recv, h_send, h_recv, g_own.at[0]
     )
     wo.start()
+    wo2 = OutputWeights(swapped, wo_far, i_send, i_recv, j_send, j_recv, i_own.at[0])
+    begin()
 
     def ring(right, k, ch, place):
         ss, rs, to = (r_send, r_recv, ring_r) if right else (l_send, l_recv, ring_l)
@@ -176,14 +182,14 @@
 
     for ch in (0, 1):
         pl.when(moves)(lambda ch=ch: remote(
-            x_hbm.at[rows(ch)], xs.at[z, rows(ch)], perm_send.at[ch], perm_recv.at[ch], grp=dst_grp, tp=dst_tp
+            x_hbm.at[rows(ch)], xs.at[spot, rows(ch)], perm_send.at[ch], perm_recv.at[ch], grp=dst_grp, tp=dst_tp
         ).wait_recv())
         pl.when(stays)(lambda ch=ch: perm_local(ch).wait())
         for right in (True, False):
-            send(ring(right, 1, ch, z))
-
-    even = z % 2 == 0
-    pair = z // 2
+            send(ring(right, 1, ch, spot))
+
+    even = spot % 2 == 0
+    pair = spot // 2
     order = [
         pair,
         jnp.where(even, pair + 3, pair + 1) % 4,
@@ -230,27 +236,34 @@
             for right in (True, False):
                 if not travels(right, k, ch):
                     continue
-                place = (z + 8 - k) % 8 if right else (z + k) % 8
+                place = (spot + 8 - k) % 8 if right else (spot + k) % 8
                 ring(right, k, ch, place).wait_recv()
                 if k < 4 and travels(right, k + 1, ch):
                     send(ring(right, k + 1, ch, place))
-        compute(0, k - 1)
-        if k > 1:
-            pass_on(0, k - 2)
+        if k < 4:
+            compute(0, k - 1)
         if k == 2:
+            pass_on(0, 0)
             wo.middle()
+        if k == 3:
+            pass_on(0, 1)
+            for copy in w_out:
+                copy.wait_recv()
+            far_cols = pl.ds(pl.multiple_of(512 * (xh ^ 1), 512), 512)
+            far = remote(wo_hbm.at[:, far_cols], swapped, f_send.at[0], f_recv.at[0], tp=tp ^ 1)
+            far.start()
+            compute(1, 0)
+            compute(1, 1)
+            pass_on(0, 2)
+            compute(1, 2)
+            wo.last()
+            pass_on(1, 0)
+            pass_on(1, 1)
+    compute(0, 3)
+    compute(1, 3)
+    pass_on(1, 2)
     pass_on(0, 3)
-    for copy in w_out:
-        copy.wait_recv()
-    far_cols = pl.ds(pl.multiple_of(512 * (xh ^ 1), 512), 512)
-    far = remote(wo_hbm.at[:, far_cols], wo_far, f_send.at[0], f_recv.at[0], tp=tp ^ 1)
-    far.start()
-    for i in range(4):
-        compute(1, i)
-        if i > 0:
-            pass_on(1, i - 1)
     pass_on(1, 3)
-    wo.last()
 
     near = c == xh
 
@@ -275,6 +288,8 @@
 
         remote(final.at[j], spot, b_send.at[j], b_recv.at[j, c], grp=2 * y + xh, tp=tp ^ 1).start()
 
+    far.wait_recv()
+    wo2.start()
     for j in (0, 1):
         spot = place_of(xh ^ j, c)
 
@@ -292,62 +307,33 @@
                     grp=2 * y + xh, tp=tp ^ 1,
                 ).wait_recv()
 
-        remote(final.at[j], spot, b_send.at[j], b_recv.at[j, c], grp=2 * y + xh, tp=tp ^ 1).wait_send()
-
-    for copy in sent:
-        copy.wait_send()
-    for copy in w_out:
-        copy.wait_send()
-    for ch in (0, 1):
-        pl.when(moves)(lambda ch=ch: perm(ch).wait_send())
-    for j in (0, 1):
-        for i in range(4):
-            d = (order[i] - y + 4) % 4
-            pl.when(d != 0)(lambda j=j, i=i, d=d: y_copy(j, i, d).wait_send())
-    wo.finish()
-    far.wait()
-
-
-def project(x, wq, wkv, wo):
-    dma = pltpu.SemaphoreType.DMA
-    anywhere = pl.BlockSpec(memory_space=pl.ANY)
-    return pl.pallas_call(
-        project_kernel,
-        out_shape=(
-            jax.ShapeDtypeStruct((2, 256, 640), BF),
-            jax.ShapeDtypeStruct((8, 512, 512), BF),
-            jax.ShapeDtypeStruct((512, 512), BF),
-        ),
-        in_specs=[anywhere] * 4,
-        out_specs=(anywhere,) * 3,
-        scratch_shapes=[
-            pltpu.VMEM((8, 256, 512), BF),
-            pltpu.VMEM((2, 1024, 640), BF),
-            pltpu.VMEM((2, 4, 128, 640), F32),
-            pltpu.VMEM((2, 128, 640), F32),
-            pltpu.VMEM((2, 4, 128, 640), BF),
-            pltpu.VMEM((2, 4, 128, 640), BF),
-            pltpu.VMEM((2, 4, 128, 640), BF),
-            pltpu.VMEM((2, 3, 128, 640), BF),
-            pltpu.VMEM((2, 128, 640), BF),
-            dma((2,)), dma((2,)), dma((4, 2)), dma((4, 2)), dma((4, 2)), dma((4, 2)), dma((2,)), dma((2,)), dma((2,)),
-            dma((2, 4)), dma((2, 4)), dma((2, 4)), dma((2, 3)), dma((2,)), dma((2,)), dma((2,)), dma((2, 2)), dma((2,)),
-            dma((4,)), dma((4,)), dma((4,)), dma((4,)), dma((1,)), dma((1,)), dma((1,)),
-        ],
-        compiler_params=pltpu.CompilerParams(
-            collective_id=0, has_side_effects=True, vmem_limit_bytes=58 * MIB
-        ),
-        name="project",
-    )(x, wq, wkv, wo)
-
-
-def attend(group, q_ref, kv_ref, len_ref, out_ref, lse_ref, q_rows, leader):
+    def drain():
+        for j in (0, 1):
+            remote(
+                final.at[j], place_of(xh ^ j, c), b_send.at[j], b_recv.at[j, c], grp=2 * y + xh, tp=tp ^ 1
+            ).wait_send()
+        for copy in sent:
+            copy.wait_send()
+        for copy in w_out:
+            copy.wait_send()
+        for ch in (0, 1):
+            pl.when(moves)(lambda ch=ch: perm(ch).wait_send())
+        for j in (0, 1):
+            for i in range(4):
+                d = (order[i] - y + 4) % 4
+                pl.when(d != 0)(lambda j=j, i=i, d=d: y_copy(j, i, d).wait_send())
+        far.wait_send()
+
+    return wo, wo2, drain
+
+
+def attend(group, q_ref, kv_ref, len_ref, out_ref, lse_ref, q_rows, xh):
     scale = HD ** -0.5
     lane = lax.broadcasted_iota(jnp.int32, (1, 128), 1)
     pos = lax.broadcasted_iota(jnp.int32, (256, 128), 0)
     lane_roll, lane_step = lane // 32, lane % 32 // 8
     new_row = lax.broadcasted_iota(jnp.int32, (16, 128), 0)
-    causal = (new_row // 4 == lane_roll) & (new_row % 4 <= lane_step) & leader
+    causal = (new_row // 4 == lane_roll) & (new_row % 4 <= lane_step) & (xh == 0)
     tokens = pl.ds(pl.multiple_of(16 * group, 16), 16)
     for part in (0, 1):
         vals = q_ref[part, tokens, :].astype(F32)
@@ -360,7 +346,10 @@
     for i in range(4):
         one = dot(kv_ref[4 * group + i, :, :128], q_t)
         cached = one if cached is None else jnp.where(lane_roll == i, one, cached)
-    visible = pos < len_ref[group]
+    span = jnp.zeros((1, 128), jnp.int32)
+    for i in range(4):
+        span = jnp.where(lane_roll == i, len_ref[4 * group + i], span)
+    visible = pos < span - 256 * xh
     cached = jnp.where(visible, cached * scale, -1e30)
     fresh = jnp.where(causal, dot(new_key, q_t) * scale, -1e30)
     peak = jnp.maximum(jnp.max(cached, axis=0, keepdims=True), jnp.max(fresh, axis=0, keepdims=True))
@@ -379,42 +368,19 @@
         out_ref[pl.ds(pl.multiple_of(128 * group + 32 * i, 32), 32), :] = got.astype(BF)
 
 
-def finish_kernel(
-    q_ref, kv_hbm, len_ref, wo_own_hbm, wo_far_hbm, head_ref, hidden_out, gap_out,
-    kv, q_rows, o_own, lse_own, o_got, lse_got, near_w, far_w, merged, ctx, outgo, income, gap_own, gaps_all,
-    kv_sem, o_send, o_recv, s_send, s_recv, near_sem, ring_send, ring_recv, gap_send, gap_recv,
-    g_send, g_recv, h_send, h_recv, g_own,
+def finish(
+    q_ref, cache_copy, len_ref, wo, wo2, head_ref, hidden_out, gap_out,
+    kv, q_rows, o_own, lse_own, o_got, lse_got, near_w, far_w, merged, ctx, outgo, income, gap_own, gap_x, gap_z,
+    o_send, o_recv, s_send, s_recv, ring_send, ring_recv, gx_send, gx_recv, gz_send, gz_recv,
 ):
     grp, tp, y, c, z, xh = places()
     sec = lax.axis_index("sec")
-    barrier = pltpu.get_barrier_semaphore()
-
-    def others():
-        for d in range(1, 32):
-            yield d - 1, dict(tp=(tp + d % 16) % 16, sec=sec ^ (d // 16))
-
-    for _, where in others():
-        pl.semaphore_signal(barrier, inc=1, device_id=where, device_id_type=MESH)
-    for away in (grp ^ 1, 2 * ((y + 1) % 4) + c, 2 * ((y + 3) % 4) + c):
-        pl.semaphore_signal(barrier, inc=1, device_id={"grp": away}, device_id_type=MESH)
-
-    def cache_copy(n):
-        rollouts = pl.ds(pl.multiple_of(8 * n, 8), 8)
-        return pltpu.make_async_copy(kv_hbm.at[rollouts], kv.at[rollouts], kv_sem.at[n])
-
-    for n in range(8):
-        cache_copy(n).start()
-    near = pltpu.make_async_copy(wo_own_hbm, near_w, near_sem.at[0])
-    near.start()
-    wo = OutputWeights(wo_far_hbm, far_w, g_send, g_recv, h_send, h_recv, g_own.at[0])
-    pl.semaphore_wait(barrier, 34)
-    wo.start()
 
     def attend_part(n):
         def body(m, carry):
             cache_copy(m).wait()
             for lane in (0, 1):
-                attend(2 * m + lane, q_ref, kv, len_ref, o_own, lse_own, q_rows.at[lane], xh == 0)
+                attend(2 * m + lane, q_ref, kv, len_ref, o_own, lse_own, q_rows.at[lane], xh)
             return carry
 
         lax.fori_loop(2 * n, 2 * n + 2, body, 0)
@@ -447,15 +413,13 @@
         attend_part(n)
         lse_copy(n).start()
         o_copy(n).start()
+        if n == 1:
+            wo2.middle()
         if n > 1:
             merge(n - 2)
-        if n == 3:
-            wo.middle()
-    merge(2)
-    merge(3)
-    near.wait()
-    wo.last()
+    wo2.last()
     wo.finish()
+    wo2.finish()
 
     def block(place, ch):
         return dot(ctx[xh, 128 * ch:128 * ch + 128, :], near_w[place]) + dot(
@@ -476,7 +440,10 @@
         return 4 if ch == (0 if right else 1) else 3
 
     for turn in range(4):
-        for right, ch in ((True, 0), (False, 1), (True, 1), (False, 0)):
+        for right, ch in ((True, 0), (False, 0), (False, 1), (True, 1)):
+            if turn == 0 and (right, ch) == (False, 1):
+                merge(2)
+                merge(3)
             k = longest(right, ch) - turn
             if k < 1:
                 continue
@@ -511,24 +478,38 @@
         gaps.append(jnp.sum(dot_nt(triple, result), axis=0, keepdims=True))
     gap = jnp.concatenate(gaps + [jnp.zeros((6, 128), F32)], axis=0)
     gap = jnp.where(sec == 0, gap, -gap)
-    own_place = 16 * sec + tp
+    own_x = 2 * xh + sec
     gap_own[...] = gap
-    gaps_all[own_place] = gap
-
-    def gap_copy(n, where):
-        return remote(gap_own, gaps_all.at[own_place], gap_send.at[n], gap_recv.at[n], **where)
-
-    for n, where in others():
-        gap_copy(n, where).start()
-    for n, where in others():
-        gap_copy(n, where).wait_recv()
-    total = gaps_all[0]
-    for n in range(1, 32):
-        total = total + gaps_all[n]
+    gap_x[own_x] = gap
+    def gap_far(d):
+        return remote(
+            gap_own, gap_x.at[own_x], gx_send.at[d - 1], gx_recv.at[d - 1], tp=tp ^ (d // 2), sec=sec ^ (d % 2)
+        )
+
+    for d in (1, 2, 3):
+        gap_far(d).start()
+    for d in (1, 2, 3):
+        gap_far(d).wait_recv()
+    gap_z[z] = gap_x[0] + gap_x[1] + gap_x[2] + gap_x[3]
+
+    def gap_ring(d):
+        return remote(
+            gap_z.at[z], gap_z.at[z], gz_send.at[d - 1], gz_recv.at[d - 1], tp=2 * ((z + d) % 8) + xh
+        )
+
+    for d in range(1, 8):
+        gap_ring(d).start()
+    for d in range(1, 8):
+        gap_ring(d).wait_recv()
+    total = gap_z[0]
+    for n in range(1, 8):
+        total = total + gap_z[n]
     gap_out[...] = total
 
-    for n, where in others():
-        gap_copy(n, where).wait_send()
+    for d in (1, 2, 3):
+        gap_far(d).wait_send()
+    for d in range(1, 8):
+        gap_ring(d).wait_send()
     for copy in sent:
         copy.wait_send()
     for n in range(4):
@@ -536,47 +517,92 @@
         o_copy(n).wait_send()
 
 
-def finish(qkv, cache, spans, wo_own, wo_far, value_head):
+def layer_kernel(
+    n_first, n_held, x_hbm, wq_hbm, wkv_hbm, wo_hbm, kv_hbm, len_ref, head_ref, hidden_out, gap_out, *scratch
+):
+    qkv, near_w, swapped, far_w, kv, kv_sem, *rest = scratch
+    first, rest = rest[:n_first], rest[n_first:]
+    held, sems = rest[:n_held], rest[n_held:]
+
+    def cache_copy(n):
+        rollouts = pl.ds(pl.multiple_of(8 * n, 8), 8)
+        return pltpu.make_async_copy(kv_hbm.at[rollouts], kv.at[rollouts], kv_sem.at[n])
+
+    def begin():
+        for n in range(8):
+            cache_copy(n).start()
+
+    wo, wo2, drain = project(x_hbm, wq_hbm, wkv_hbm, wo_hbm, qkv, near_w, swapped, far_w, begin, *first)
+    q_rows, o_own, lse_own, o_got, lse_got, *after = held
+    finish(
+        qkv, cache_copy, len_ref, wo, wo2, head_ref, hidden_out, gap_out,
+        kv, q_rows, o_own, lse_own, o_got, lse_got, near_w, far_w, *after, *sems,
+    )
+    drain()
+
+
+def layer(x, wq, wkv, wo, cache, lengths, value_head):
     dma = pltpu.SemaphoreType.DMA
     anywhere = pl.BlockSpec(memory_space=pl.ANY)
     vmem = pl.BlockSpec(memory_space=pltpu.VMEM)
+    shared = [
+        pltpu.VMEM((2, 256, 640), BF),
+        pltpu.VMEM((8, 512, 512), BF),
+        pltpu.VMEM((512, 512), BF),
+        pltpu.VMEM((8, 512, 512), BF),
+        pltpu.VMEM((64, 256, 256), BF),
+        dma((8,)),
+    ]
+    first = [
+        pltpu.VMEM((8, 256, 512), BF),
+        pltpu.VMEM((2, 1024, 640), BF),
+        pltpu.VMEM((2, 4, 128, 640), F32),
+        pltpu.VMEM((2, 128, 640), F32),
+        pltpu.VMEM((2, 4, 128, 640), BF),
+        pltpu.VMEM((2, 4, 128, 640), BF),
+        pltpu.VMEM((2, 4, 128, 640), BF),
+        pltpu.VMEM((2, 3, 128, 640), BF),
+        pltpu.VMEM((2, 128, 640), BF),
+        dma((2,)), dma((2,)), dma((4, 2)), dma((4, 2)), dma((4, 2)), dma((4, 2)), dma((2,)), dma((2,)), dma((2,)),
+        dma((2, 4)), dma((2, 4)), dma((2, 4)), dma((2, 3)), dma((2,)), dma((2,)), dma((2,)), dma((2, 2)), dma((2,)),
+        dma((4,)), dma((4,)), dma((4,)), dma((4,)), dma((1,)), dma((1,)), dma((1,)),
+        dma((4,)), dma((4,)), dma((4,)), dma((4,)), dma((1,)),
+    ]
+    held = [
+        pltpu.VMEM((2, 128, 128), F32),
+        pltpu.VMEM((2048, 128), BF),
+        pltpu.VMEM((16, 1, 128), F32),
+        pltpu.VMEM((2048, 128), BF),
+        pltpu.VMEM((16, 1, 128), F32),
+        pltpu.VMEM((2048, 128), F32),
+        pltpu.VMEM((2, 256, 512), BF),
+        pltpu.VMEM((4, 4, 128, 512), BF),
+        pltpu.VMEM((4, 4, 128, 512), BF),
+        pltpu.VMEM((8, 128), F32),
+        pltpu.VMEM((4, 8, 128), F32),
+        pltpu.VMEM((8, 8, 128), F32),
+    ]
+    sems = [
+        dma((4,)), dma((4,)), dma((4,)), dma((4,)), dma((4, 4)), dma((4, 4)), dma((3,)), dma((3,)), dma((7,)), dma((7,)),
+    ]
     return pl.pallas_call(
-        finish_kernel,
+        functools.partial(layer_kernel, len(first), len(held)),
         out_shape=(jax.ShapeDtypeStruct((256, 512), BF), jax.ShapeDtypeStruct((8, 128), F32)),
-        in_specs=[vmem, anywhere, vmem, anywhere, anywhere, vmem],
+        in_specs=[anywhere] * 5 + [pl.BlockSpec(memory_space=pltpu.SMEM), vmem],
         out_specs=(vmem, vmem),
-        scratch_shapes=[
-            pltpu.VMEM((64, 256, 256), BF),
-            pltpu.VMEM((2, 128, 128), F32),
-            pltpu.VMEM((2048, 128), BF),
-            pltpu.VMEM((16, 1, 128), F32),
-            pltpu.VMEM((2048, 128), BF),
-            pltpu.VMEM((16, 1, 128), F32),
-            pltpu.VMEM((8, 512, 512), BF),
-            pltpu.VMEM((8, 512, 512), BF),
-            pltpu.VMEM((2048, 128), F32),
-            pltpu.VMEM((2, 256, 512), BF),
-            pltpu.VMEM((4, 4, 128, 512), BF),
-            pltpu.VMEM((4, 4, 128, 512), BF),
-            pltpu.VMEM((8, 128), F32),
-            pltpu.VMEM((32, 8, 128), F32),
-            dma((8,)), dma((4,)), dma((4,)), dma((4,)), dma((4,)), dma((1,)),
-            dma((4, 4)), dma((4, 4)), dma((31,)), dma((31,)),
-            dma((4,)), dma((4,)), dma((4,)), dma((4,)), dma((1,)),
-        ],
+        scratch_shapes=shared + first + held + sems,
         compiler_params=pltpu.CompilerParams(
-            collective_id=1, has_side_effects=True, vmem_limit_bytes=58 * MIB
+            collective_id=0, has_side_effects=True, vmem_limit_bytes=60 * MIB
         ),
-        name="finish",
-    )(qkv, cache, spans, wo_own, wo_far, value_head)
+        name="layer",
+    )(x, wq, wkv, wo, cache, lengths, value_head)
 
 
 def local(layer_in, q_weight, kv_weight, o_weight, kv_cache, cache_lengths, value_head):
-    xh = lax.axis_index("tp") % 2
     x = layer_in[0].reshape(256, 512)
-    qkv, wo_own, wo_far = project(x, q_weight[0], kv_weight[0], o_weight[0])
-    spans = jnp.repeat(cache_lengths - xh * 256, 32).reshape(16, 1, 128)
-    hidden, gap = finish(qkv, kv_cache[0], spans, wo_own, wo_far, value_head.reshape(1, 512))
+    hidden, gap = layer(
+        x, q_weight[0], kv_weight[0], o_weight[0], kv_cache[0], cache_lengths, value_head.reshape(1, 512)
+    )
     hidden_out = hidden.reshape(1, 64, 4, 512)
     own_gap = lax.dynamic_slice_in_dim(gap[:2].reshape(64, 4), 2 * lax.axis_index("sec"), 2, 1)
     return hidden_out, own_gap

time: 150 us -> 131 us (0.87)
  Pallas kernels: 142 us -> 125 us
    pallas_call x2 -> x1, Pallas kernels: 142 us -> 125 us  [layer(): pl.pallas_call(functools.partial(layer_kernel, len(first), len(held)), ou...]
where the time goes in v4:
time: 131 us
  Pallas kernels  125 us (95%)
  local copies, waits for them, and re-layouts  4.94 us (4%)
    pallas_call x1, Pallas kernels, layer(): pl.pallas_call(functools.partial(layer_kernel, len(first), len(held)), ou...  125 us

profile of v4, /device:TPU:8, one launch (start us, length us, event | category | flops | bytes accessed | tf_op | source)
XLA Modules:
  0.0 130.9 jit_solution(527166201933796793)
XLA Ops:
  0.6 1.7 %reshape_squeeze.3.x_hbm = bf16[256,512]{1,0:T(8,128)(2,1)} reshape(bf16[1,64,4,512]{3,2,1,0:T(4,128)(2,1)} %param.7) | data formatting | bytes 524288 | tf_op jit(solution)/shard_map/reshape;squeeze | solution.py:602
  2.3 125.3 %layer.1 = (bf16[256,512]{1,0:T(8,128)(2,1)}, f32[8,128]{1,0:T(8,128)}) custom-call(bf16[256,512]{1,0:T(8,128)(2,1)} %reshape_squeeze.3.x_hbm, bf16[1024,512]{1,0:T(8,128)(2,1)} %bitcast.6, bf16[1024,128]{1,0:T(8,128)(2,1)} %bitcast.8, bf16[512,1024]{1,0:T(8,128)(2,1)} %bitcast.7, bf16[64,256,256]{2,1,0:T(8,128)(2,1)} %bitcast.5, s32[64]{0:T(128)} %len_ref.1, ...), custom_call_target="tpu_custom_call" | custom-call | tf_op jit(solution)/shard_map/layer/pallas_call | solution.py:588
  127.7 1.7 %reshape.14 = bf16[1,64,4,512]{3,2,1,0:T(4,128)(2,1)} reshape(bf16[256,512]{1,0:T(8,128)(2,1)} %get-tuple-element.4) | data formatting | bytes 524288 | tf_op jit(solution)/shard_map/reshape | solution.py:606
  129.4 0.7 slice.3
  130.1 0.1 reshape.15
  130.2 0.1 constant_dynamic-slice_fusion
  130.3 0.6 copy.10

commit v5 on v4

--- a/solution.py
+++ b/solution.py
@@ -17,10 +17,6 @@
 
 def dot(a, b):
     return jnp.dot(a, b, preferred_element_type=F32)
-
-
-def dot_nt(a, b):
-    return lax.dot_general(a, b, (((1,), (1,)), ((), ())), preferred_element_type=F32)
 
 
 def remote(src, dst, send, recv, **where):
@@ -98,7 +94,7 @@
 
 
 def project(
-    x_hbm, wq_hbm, wkv_hbm, wo_hbm, qkv_out, wo_own, swapped, wo_far, begin,
+    x_hbm, wq_hbm, wkv_hbm, wo_hbm, qkv_out, wo_own, swapped, wo_far, prepare, begin,
     xs, ws, mine, keep, to_core, from_core, to_y, from_y, final,
     perm_send, perm_recv, r_send, r_recv, l_send, l_recv, w_local, w_send, w_recv,
     c_send, c_recv, y_send, y_recv, a_send, a_recv, b_send, b_recv, own_sem,
@@ -132,6 +128,7 @@
     greet(grp=grp ^ 1, tp=tp ^ 1)
     for d in (1, 2, 3):
         greet(grp=2 * ((y + d) % 4) + c)
+    prepare()
     pl.semaphore_wait(barrier, jnp.where(moves, 17, 15))
 
     def rows(ch):
@@ -275,6 +272,9 @@
         for d in (1, 2, 3):
             remote(to_y.at[j, 0], from_y.at[j, d - 1], y_send.at[j, 0], y_recv.at[j, d - 1], grp=grp).wait_recv()
             total = total + from_y[j, d - 1].astype(F32)
+        if j == 1:
+            far.wait_recv()
+            wo2.start()
         final[j] = total.astype(BF)
         spot = place_of(xh ^ j, c)
 
@@ -288,8 +288,6 @@
 
         remote(final.at[j], spot, b_send.at[j], b_recv.at[j, c], grp=2 * y + xh, tp=tp ^ 1).start()
 
-    far.wait_recv()
-    wo2.start()
     for j in (0, 1):
         spot = place_of(xh ^ j, c)
 
@@ -369,8 +367,8 @@
 
 
 def finish(
-    q_ref, cache_copy, len_ref, wo, wo2, head_ref, hidden_out, gap_out,
-    kv, q_rows, o_own, lse_own, o_got, lse_got, near_w, far_w, merged, ctx, outgo, income, gap_own, gap_x, gap_z,
+    q_ref, cache_copy, len_ref, wo, wo2, heads, head_copy, hidden_out, gap_out,
+    kv, q_rows, o_own, lse_own, o_got, lse_got, near_w, far_w, merged, ctx, outgo, income, terms, gap_part, gap_own, gap_x, gap_z,
     o_send, o_recv, s_send, s_recv, ring_send, ring_recv, gx_send, gx_recv, gz_send, gz_recv,
 ):
     grp, tp, y, c, z, xh = places()
@@ -420,11 +418,21 @@
     wo2.last()
     wo.finish()
     wo2.finish()
+    for d in range(1, 8):
+        head_copy(d).wait_recv()
+
+    gap_part[...] = jnp.zeros_like(gap_part)
 
     def block(place, ch):
-        return dot(ctx[xh, 128 * ch:128 * ch + 128, :], near_w[place]) + dot(
+        total = dot(ctx[xh, 128 * ch:128 * ch + 128, :], near_w[place]) + dot(
             ctx[xh ^ 1, 128 * ch:128 * ch + 128, :], far_w[place]
         )
+        valued = total * heads[place]
+        gap_part[ch] += valued[:, :128] + valued[:, 128:256] + valued[:, 256:384] + valued[:, 384:]
+        return total
+
+    def place_at(right, k):
+        return (z + k) % 8 if right else (z + 8 - k) % 8
 
     def slot(right, ch):
         return 2 * ch + (0 if right else 1)
@@ -439,72 +447,72 @@
     def longest(right, ch):
         return 4 if ch == (0 if right else 1) else 3
 
-    for turn in range(4):
-        for right, ch in ((True, 0), (False, 0), (False, 1), (True, 1)):
-            if turn == 0 and (right, ch) == (False, 1):
-                merge(2)
-                merge(3)
-            k = longest(right, ch) - turn
-            if k < 1:
-                continue
-            place = (z + k) % 8 if right else (z + 8 - k) % 8
-            total = block(place, ch)
-            if turn > 0:
-                ring(right, ch, k + 1).wait_recv()
-                total = total + income[slot(right, ch), k].astype(F32)
-            outgo[slot(right, ch), k - 1] = total.astype(BF)
-            copy = ring(right, ch, k)
-            copy.start()
-            sent.append(copy)
-
-    value = head_ref[...]
-    first = value.astype(BF)
-    rest = value - first.astype(F32)
-    second = rest.astype(BF)
-    third = (rest - second.astype(F32)).astype(BF)
-    which = lax.broadcasted_iota(jnp.int32, (16, 512), 0)
-    triple = jnp.where(
-        which == 0, first.astype(F32),
-        jnp.where(which == 1, second.astype(F32), jnp.where(which == 2, third.astype(F32), 0.0)),
-    ).astype(BF)
-    gaps = []
+    streams = ((True, 0), (False, 0), (False, 1), (True, 1))
+
+    def push(right, ch, k, total):
+        outgo[slot(right, ch), k - 1] = total.astype(BF)
+        copy = ring(right, ch, k)
+        copy.start()
+        sent.append(copy)
+
+    for right, ch in streams:
+        if (right, ch) == (False, 1):
+            merge(2)
+            merge(3)
+        k = longest(right, ch)
+        push(right, ch, k, block(place_at(right, k), ch))
     for ch in (0, 1):
-        total = block(z, ch)
         for right in (True, False):
-            ring(right, ch, 1).wait_recv()
-            total = total + income[slot(right, ch), 0].astype(F32)
-        result = total.astype(BF)
-        hidden_out[128 * ch:128 * ch + 128, :] = result
-        gaps.append(jnp.sum(dot_nt(triple, result), axis=0, keepdims=True))
-    gap = jnp.concatenate(gaps + [jnp.zeros((6, 128), F32)], axis=0)
+            for k in range(longest(right, ch) - 1, 0, -1):
+                place = place_at(right, k)
+                terms[ch, place] = block(place, ch)
+        terms[ch, z] = block(z, ch)
+
+    gap = jnp.concatenate(
+        [jnp.sum(gap_part[ch].T, axis=0, keepdims=True) for ch in (0, 1)] + [jnp.zeros((6, 128), F32)], axis=0
+    )
     gap = jnp.where(sec == 0, gap, -gap)
     own_x = 2 * xh + sec
     gap_own[...] = gap
     gap_x[own_x] = gap
+
     def gap_far(d):
         return remote(
             gap_own, gap_x.at[own_x], gx_send.at[d - 1], gx_recv.at[d - 1], tp=tp ^ (d // 2), sec=sec ^ (d % 2)
         )
 
-    for d in (1, 2, 3):
-        gap_far(d).start()
-    for d in (1, 2, 3):
-        gap_far(d).wait_recv()
-    gap_z[z] = gap_x[0] + gap_x[1] + gap_x[2] + gap_x[3]
-
     def gap_ring(d):
         return remote(
             gap_z.at[z], gap_z.at[z], gz_send.at[d - 1], gz_recv.at[d - 1], tp=2 * ((z + d) % 8) + xh
         )
 
-    for d in range(1, 8):
-        gap_ring(d).start()
+    for d in (1, 2, 3):
+        gap_far(d).start()
+    for turn in (1, 2, 3):
+        for right, ch in streams:
+            k = longest(right, ch) - turn
+            if k < 1:
+                continue
+            ring(right, ch, k + 1).wait_recv()
+            push(right, ch, k, terms[ch, place_at(right, k)] + income[slot(right, ch), k].astype(F32))
+        if turn == 1:
+            for d in (1, 2, 3):
+                gap_far(d).wait_recv()
+            gap_z[z] = gap_x[0] + gap_x[1] + gap_x[2] + gap_x[3]
+            for d in range(1, 8):
+                gap_ring(d).start()
     for d in range(1, 8):
         gap_ring(d).wait_recv()
     total = gap_z[0]
     for n in range(1, 8):
         total = total + gap_z[n]
     gap_out[...] = total
+    for ch in (0, 1):
+        total = terms[ch, z]
+        for right in (True, False):
+            ring(right, ch, 1).wait_recv()
+            total = total + income[slot(right, ch), 0].astype(F32)
+        hidden_out[32 * ch:32 * ch + 32] = total.reshape(32, 4, 512).astype(BF)
 
     for d in (1, 2, 3):
         gap_far(d).wait_send()
@@ -520,7 +528,8 @@
 def layer_kernel(
     n_first, n_held, x_hbm, wq_hbm, wkv_hbm, wo_hbm, kv_hbm, len_ref, head_ref, hidden_out, gap_out, *scratch
 ):
-    qkv, near_w, swapped, far_w, kv, kv_sem, *rest = scratch
+    qkv, near_w, swapped, far_w, kv, kv_sem, heads, v_send, v_recv, x_split, x_flat, x_sem, *rest = scratch
+    grp, tp, y, c, z, xh = places()
     first, rest = rest[:n_first], rest[n_first:]
     held, sems = rest[:n_held], rest[n_held:]
 
@@ -528,17 +537,31 @@
         rollouts = pl.ds(pl.multiple_of(8 * n, 8), 8)
         return pltpu.make_async_copy(kv_hbm.at[rollouts], kv.at[rollouts], kv_sem.at[n])
 
+    def head_copy(d):
+        return remote(head_ref, heads.at[z], v_send.at[d - 1], v_recv.at[d - 1], tp=2 * ((z + d) % 8) + xh)
+
     def begin():
         for n in range(8):
             cache_copy(n).start()
-
-    wo, wo2, drain = project(x_hbm, wq_hbm, wkv_hbm, wo_hbm, qkv, near_w, swapped, far_w, begin, *first)
+        for d in range(1, 8):
+            head_copy(d).start()
+        heads[z] = head_ref[...]
+
+    def prepare():
+        load = pltpu.make_async_copy(x_hbm, x_split, x_sem.at[0])
+        load.start()
+        load.wait()
+        x_flat[...] = x_split[...].astype(F32).reshape(256, 512).astype(BF)
+
+    wo, wo2, drain = project(x_flat, wq_hbm, wkv_hbm, wo_hbm, qkv, near_w, swapped, far_w, prepare, begin, *first)
     q_rows, o_own, lse_own, o_got, lse_got, *after = held
     finish(
-        qkv, cache_copy, len_ref, wo, wo2, head_ref, hidden_out, gap_out,
+        qkv, cache_copy, len_ref, wo, wo2, heads, head_copy, hidden_out, gap_out,
         kv, q_rows, o_own, lse_own, o_got, lse_got, near_w, far_w, *after, *sems,
     )
     drain()
+    for d in range(1, 8):
+        head_copy(d).wait_send()
 
 
 def layer(x, wq, wkv, wo, cache, lengths, value_head):
@@ -552,6 +575,11 @@
         pltpu.VMEM((8, 512, 512), BF),
         pltpu.VMEM((64, 256, 256), BF),
         dma((8,)),
+        pltpu.VMEM((8, 1, 512), F32),
+        dma((7,)), dma((7,)),
+        pltpu.VMEM((64, 4, 512), BF),
+        pltpu.VMEM((256, 512), BF),
+        dma((1,)),
     ]
     first = [
         pltpu.VMEM((8, 256, 512), BF),
@@ -578,6 +606,8 @@
         pltpu.VMEM((2, 256, 512), BF),
         pltpu.VMEM((4, 4, 128, 512), BF),
         pltpu.VMEM((4, 4, 128, 512), BF),
+        pltpu.VMEM((2, 8, 128, 512), F32),
+        pltpu.VMEM((2, 128, 128), F32),
         pltpu.VMEM((8, 128), F32),
         pltpu.VMEM((4, 8, 128), F32),
         pltpu.VMEM((8, 8, 128), F32),
@@ -587,7 +617,7 @@
     ]
     return pl.pallas_call(
         functools.partial(layer_kernel, len(first), len(held)),
-        out_shape=(jax.ShapeDtypeStruct((256, 512), BF), jax.ShapeDtypeStruct((8, 128), F32)),
+        out_shape=(jax.ShapeDtypeStruct((64, 4, 512), BF), jax.ShapeDtypeStruct((8, 128), F32)),
         in_specs=[anywhere] * 5 + [pl.BlockSpec(memory_space=pltpu.SMEM), vmem],
         out_specs=(vmem, vmem),
         scratch_shapes=shared + first + held + sems,
@@ -599,11 +629,10 @@
 
 
 def local(layer_in, q_weight, kv_weight, o_weight, kv_cache, cache_lengths, value_head):
-    x = layer_in[0].reshape(256, 512)
     hidden, gap = layer(
-        x, q_weight[0], kv_weight[0], o_weight[0], kv_cache[0], cache_lengths, value_head.reshape(1, 512)
+        layer_in[0], q_weight[0], kv_weight[0], o_weight[0], kv_cache[0], cache_lengths, value_head.reshape(1, 512)
     )
-    hidden_out = hidden.reshape(1, 64, 4, 512)
+    hidden_out = hidden[None]
     own_gap = lax.dynamic_slice_in_dim(gap[:2].reshape(64, 4), 2 * lax.axis_index("sec"), 2, 1)
     return hidden_out, own_gap
 

time: 131 us -> 121 us (0.924); the launches traced: 131 us -> 119 us
  Pallas kernels: 125 us -> 115 us
  local copies, waits for them, and re-layouts: 4.94 us -> 3.25 us
    pallas_call x1, Pallas kernels: 125 us -> 115 us  [layer(): pl.pallas_call(functools.partial(layer_kernel, len(first), len(held)), ou...]
    unnamed x1 -> x2, local copies, waits for them, and re-layouts: 0.64 us -> 2.39 us
    reshape x1 -> x0, local copies, waits for them, and re-layouts: 1.72 us -> none  [local(): hidden_out = hidden.reshape(1, 64, 4, 512)]
    another operation x1 -> x0, local copies, waits for them, and re-layouts: 1.72 us -> none  [local(): x = layer_in[0].reshape(256, 512)]
where the time goes in v5:
time: 121 us; the launch traced here: 119 us
  Pallas kernels  115 us (95%)
  local copies, waits for them, and re-layouts  3.25 us (3%)
    pallas_call x1, Pallas kernels, layer(): pl.pallas_call(functools.partial(layer_kernel, len(first), len(held)), ou...  115 us

profile of v5, /device:TPU:8, one launch (start us, length us, event | category | flops | bytes accessed | tf_op | source)
XLA Modules:
  0.0 119.4 jit_solution(17961117329009458393)
XLA Ops:
  0.6 115.5 %layer.1 = (bf16[64,4,512]{2,1,0:T(4,128)(2,1)}, f32[8,128]{1,0:T(8,128)}) custom-call(bf16[64,4,512]{2,1,0:T(4,128)(2,1)} %bitcast.10, bf16[1024,512]{1,0:T(8,128)(2,1)} %bitcast.8, bf16[1024,128]{1,0:T(8,128)(2,1)} %bitcast.11, bf16[512,1024]{1,0:T(8,128)(2,1)} %bitcast.9, bf16[64,256,256]{2,1,0:T(8,128)(2,1)} %bitcast.7, s32[64]{0:T(128)} %len_ref.1, ...), custom_call_target="tpu_custom_call" | custom-call | tf_op jit(solution)/shard_map/layer/pallas_call | solution.py:618
  116.1 0.7 slice.3
  116.8 0.1 reshape.11
  116.9 0.1 constant_dynamic-slice_fusion
  117.0 0.6 copy.10
  117.7 1.7 %copy.12 = bf16[1,64,4,512]{3,2,1,0:T(4,128)(2,1)} copy(bf16[1,64,4,512]{3,2,1,0:T(4,128)(2,1)} %bitcast.12) | data formatting | bytes 524288

commit v6 on v5

--- a/solution.py
+++ b/solution.py
@@ -261,6 +261,8 @@
     pass_on(1, 2)
     pass_on(0, 3)
     pass_on(1, 3)
+    far.wait_recv()
+    wo2.start()
 
     near = c == xh
 
@@ -272,9 +274,6 @@
         for d in (1, 2, 3):
             remote(to_y.at[j, 0], from_y.at[j, d - 1], y_send.at[j, 0], y_recv.at[j, d - 1], grp=grp).wait_recv()
             total = total + from_y[j, d - 1].astype(F32)
-        if j == 1:
-            far.wait_recv()
-            wo2.start()
         final[j] = total.astype(BF)
         spot = place_of(xh ^ j, c)
 

time: 121 us -> 121 us (level)
  no operation moved by 1% of the time
where the time goes in v6:
time: 121 us; the launch traced here: 119 us
  Pallas kernels  116 us (96%)
  local copies, waits for them, and re-layouts  3.25 us (3%)
    pallas_call x1, Pallas kernels, layer(): pl.pallas_call(functools.partial(layer_kernel, len(first), len(held)), ou...  116 us

profile of v6, /device:TPU:8, one launch (start us, length us, event | category | flops | bytes accessed | tf_op | source)
XLA Modules:
  0.0 119.5 jit_solution(10344123579693239347)
XLA Ops:
  0.6 115.5 %layer.1 = (bf16[64,4,512]{2,1,0:T(4,128)(2,1)}, f32[8,128]{1,0:T(8,128)}) custom-call(bf16[64,4,512]{2,1,0:T(4,128)(2,1)} %bitcast.10, bf16[1024,512]{1,0:T(8,128)(2,1)} %bitcast.8, bf16[1024,128]{1,0:T(8,128)(2,1)} %bitcast.11, bf16[512,1024]{1,0:T(8,128)(2,1)} %bitcast.9, bf16[64,256,256]{2,1,0:T(8,128)(2,1)} %bitcast.7, s32[64]{0:T(128)} %len_ref.1, ...), custom_call_target="tpu_custom_call" | custom-call | tf_op jit(solution)/shard_map/layer/pallas_call | solution.py:617
  116.2 0.7 slice.3
  116.9 0.1 reshape.11
  117.0 0.1 constant_dynamic-slice_fusion
  117.1 0.6 copy.10
  117.7 1.7 %copy.12 = bf16[1,64,4,512]{3,2,1,0:T(4,128)(2,1)} copy(bf16[1,64,4,512]{3,2,1,0:T(4,128)(2,1)} %bitcast.12) | data formatting | bytes 524288

commit v7 on v6

--- a/solution.py
+++ b/solution.py
@@ -159,7 +159,6 @@
     wo = OutputWeights(
         wo_hbm.at[:, pl.ds(pl.multiple_of(512 * xh, 512), 512)], wo_own, g_send, g_recv, h_send, h_recv, g_own.at[0]
     )
-    wo.start()
     wo2 = OutputWeights(swapped, wo_far, i_send, i_recv, j_send, j_recv, i_own.at[0])
     begin()
 
@@ -185,6 +184,7 @@
         for right in (True, False):
             send(ring(right, 1, ch, spot))
 
+    wo.start()
     even = spot % 2 == 0
     pair = spot // 2
     order = [

time: 121 us -> 121 us (level)
  no operation moved by 1% of the time
where the time goes in v7:
time: 121 us; the launch traced here: 119 us
  Pallas kernels  116 us (96%)
  local copies, waits for them, and re-layouts  3.25 us (3%)
    pallas_call x1, Pallas kernels, layer(): pl.pallas_call(functools.partial(layer_kernel, len(first), len(held)), ou...  116 us

profile of v7, /device:TPU:8, one launch (start us, length us, event | category | flops | bytes accessed | tf_op | source)
XLA Modules:
  0.0 119.5 jit_solution(6809537860102846180)
XLA Ops:
  0.6 115.5 %layer.1 = (bf16[64,4,512]{2,1,0:T(4,128)(2,1)}, f32[8,128]{1,0:T(8,128)}) custom-call(bf16[64,4,512]{2,1,0:T(4,128)(2,1)} %bitcast.10, bf16[1024,512]{1,0:T(8,128)(2,1)} %bitcast.8, bf16[1024,128]{1,0:T(8,128)(2,1)} %bitcast.11, bf16[512,1024]{1,0:T(8,128)(2,1)} %bitcast.9, bf16[64,256,256]{2,1,0:T(8,128)(2,1)} %bitcast.7, s32[64]{0:T(128)} %len_ref.1, ...), custom_call_target="tpu_custom_call" | custom-call | tf_op jit(solution)/shard_map/layer/pallas_call | solution.py:617
  116.2 0.7 slice.3
  116.9 0.1 reshape.11
  117.0 0.1 constant_dynamic-slice_fusion
  117.1 0.6 copy.10
  117.7 1.7 %copy.12 = bf16[1,64,4,512]{3,2,1,0:T(4,128)(2,1)} copy(bf16[1,64,4,512]{3,2,1,0:T(4,128)(2,1)} %bitcast.12) | data formatting | bytes 524288
